TPU v7x, 32 devices: a whole 2x2x4 slice. The times are simulated.
32 devices in a mesh: grp: 8 (over z, y), seq: 4 (over x, core).
Axes of the slice: x: 2, y: 2, z: 4, core: 2. Of those that a mesh axis runs over, the one named last changes fastest.
Arguments:
- tokens_in: bfloat16 [24576, 768], P(('grp', 'seq')), may hold values from -6 to 6
- lengths: int32 [8], P('grp'), may hold values from 2305 to 3072, as said below
- ln1_gain: float32 [768], replicated, may hold values from 0.5 to 1.5
- ln1_bias: float32 [768], replicated, may hold values from -1.75 to 1.75
- w_qkv: bfloat16 [768, 2304], replicated, may hold values from -0.21875 to 0.21875
- bias_query: float32 [768], replicated, may hold values from -1.75 to 1.75
- bias_value: float32 [768], replicated, may hold values from -1.75 to 1.75
- w_out: bfloat16 [768, 768], replicated, may hold values from -0.875 to 0.875
- bias_out: float32 [768], replicated, may hold values from -1.75 to 1.75
- ln2_gain: float32 [768], replicated, may hold values from 0.5 to 1.5
- ln2_bias: float32 [768], replicated, may hold values from -1.75 to 1.75
- w_up: bfloat16 [768, 3072], replicated, may hold values from -0.21875 to 0.21875
- bias_up: float32 [3072], replicated, may hold values from -1.75 to 1.75
- w_down: bfloat16 [3072, 768], replicated, may hold values from -0.109375 to 0.109375
- bias_down: float32 [768], replicated, may hold values from -1.75 to 1.75
- proj_patch: bfloat16 [768, 768], replicated, may hold values from -0.21875 to 0.21875
- proj_class: bfloat16 [768, 768], replicated, may hold values from -0.21875 to 0.21875
- class_emb: bfloat16 [150, 768], replicated, may hold values from -6 to 6
- d_masks: bfloat16 [24576, 150], P(('grp', 'seq')), may hold values from -6 to 6
Outputs:
- masks: bfloat16 [24576, 150], P(('grp', 'seq'))
- grad_tokens: bfloat16 [24576, 768], P(('grp', 'seq'))
- grad_ln1_gain: float32 [768], P('grp')
- grad_ln1_bias: float32 [768], P('grp')
- grad_w_qkv: float32 [768, 2304], P('grp', 'seq')
- grad_bias_query: float32 [768], P('grp')
- grad_bias_value: float32 [768], P('grp')
- grad_w_out: float32 [768, 768], P('grp', 'seq')
- grad_bias_out: float32 [768], P('grp')
- grad_ln2_gain: float32 [768], P('grp')
- grad_ln2_bias: float32 [768], P('grp')
- grad_w_up: float32 [768, 3072], P('grp', 'seq')
- grad_bias_up: float32 [3072], P('grp')
- grad_w_down: float32 [3072, 768], P('grp', 'seq')
- grad_bias_down: float32 [768], P('grp')
- grad_proj_patch: float32 [768, 768], P('grp', 'seq')
- grad_proj_class: float32 [768, 768], P('grp', 'seq')
- grad_class_emb: float32 [150, 768], P(None, 'grp')
Inputs may be any that keep to these rules, and one draw needn't show every extreme that they name: Image g fills the first lengths[g] rows of its 3072 rows, the rest is padding; in every draw some image has exactly 3072 rows.
All inputs are finite; a program needn't handle non-finite values.
Results may differ from a plain program's by a relative error of at most 0.015.
Values may be sent and summed in bfloat16 or wider, within the bound.
A program may use at most 256 MiB of HBM per device.

v0:
```python
import math

import jax
import jax.numpy as jnp
from jax import lax
from jax.sharding import PartitionSpec as P

HEAD_DIM = 64


EPS_NORM = 1e-06
EPS_UNIT = 1e-06
NEG_FILL = -1e30


def layer_norm(matrix_rows, gain_vec, shift_vec):
    row_mean = jnp.mean(matrix_rows, axis=-1, keepdims=True)
    centred = matrix_rows - row_mean
    row_var = jnp.mean(centred * centred, axis=-1, keepdims=True)
    return centred * lax.rsqrt(row_var + EPS_NORM) * gain_vec + shift_vec


def unit_rows(matrix_rows):
    return matrix_rows * lax.rsqrt(
        jnp.sum(matrix_rows * matrix_rows, axis=-1, keepdims=True) + EPS_UNIT
    )


def gelu_exact(values_in):
    return jax.nn.gelu(values_in, approximate=False)


def score_block(query_heads, key_block, keep_block, score_scale):
    scores = (
        jnp.einsum("qhd,khd->hqk", query_heads, key_block, preferred_element_type=jnp.float32)
        * score_scale
    )
    return jnp.where(keep_block[None, None, :], scores, NEG_FILL)


def split_blocks(key_heads, value_heads, key_keep, key_span):
    block_count = key_heads.shape[0] // key_span
    head_count = key_heads.shape[1]
    key_blocks = key_heads.reshape(block_count, key_span, head_count, -1)
    value_blocks = value_heads.reshape(block_count, key_span, head_count, -1)
    keep_blocks = key_keep.reshape(block_count, key_span)
    return (key_blocks, value_blocks, keep_blocks)


def attend_forward(query_heads, key_heads, value_heads, key_keep, score_scale, key_span):
    row_count, head_count = (query_heads.shape[0], query_heads.shape[1])
    key_blocks, value_blocks, keep_blocks = split_blocks(key_heads, value_heads, key_keep, key_span)

    def gather_stats(carried, pieces):
        row_top, row_total = carried
        key_block, keep_block = pieces
        scores = score_block(query_heads, key_block, keep_block, score_scale)
        new_top = jnp.maximum(row_top, jnp.max(scores, axis=-1))
        row_total = row_total * jnp.exp(row_top - new_top) + jnp.sum(
            jnp.exp(scores - new_top[..., None]), axis=-1
        )
        return ((new_top, row_total), None)

    start_stats = (
        jnp.full((head_count, row_count), NEG_FILL, jnp.float32),
        jnp.zeros((head_count, row_count), jnp.float32),
    )
    row_top, row_total = lax.scan(gather_stats, start_stats, (key_blocks, keep_blocks))[0]
    log_mass = row_top + jnp.log(row_total)

    def weigh_values(summed, pieces):
        key_block, value_block, keep_block = pieces
        scores = score_block(query_heads, key_block, keep_block, score_scale)
        prob_low = jnp.exp(scores - log_mass[..., None]).astype(jnp.bfloat16)
        summed = summed + jnp.einsum(
            "hqk,khd->qhd", prob_low, value_block, preferred_element_type=jnp.float32
        )
        return (summed, None)

    start_sum = jnp.zeros(query_heads.shape, jnp.float32)
    attended = lax.scan(weigh_values, start_sum, (key_blocks, value_blocks, keep_blocks))[0]
    return (attended, log_mass)


def attend_backward(
    query_heads,
    key_heads,
    value_heads,
    key_keep,
    grad_heads,
    log_mass,
    attended,
    score_scale,
    key_span,
):
    head_count = query_heads.shape[1]
    key_blocks, value_blocks, keep_blocks = split_blocks(key_heads, value_heads, key_keep, key_span)
    row_delta = jnp.einsum("qhd,qhd->hq", grad_heads.astype(jnp.float32), attended)

    def spread_grads(grad_query, pieces):
        key_block, value_block, keep_block = pieces
        prob_rows = jnp.exp(
            score_block(query_heads, key_block, keep_block, score_scale) - log_mass[..., None]
        )
        grad_probs = jnp.einsum(
            "qhd,khd->hqk", grad_heads, value_block, preferred_element_type=jnp.float32
        )
        grad_scores = (prob_rows * (grad_probs - row_delta[..., None])).astype(jnp.bfloat16)
        grad_query = grad_query + jnp.einsum(
            "hqk,khd->qhd", grad_scores, key_block, preferred_element_type=jnp.float32
        )
        grad_key_block = (
            jnp.einsum("hqk,qhd->khd", grad_scores, query_heads, preferred_element_type=jnp.float32)
            * score_scale
        )
        grad_value_block = jnp.einsum(
            "hqk,qhd->khd",
            prob_rows.astype(jnp.bfloat16),
            grad_heads,
            preferred_element_type=jnp.float32,
        )
        return (grad_query, (grad_key_block, grad_value_block))

    start_query = jnp.zeros(query_heads.shape, jnp.float32)
    grad_query, block_grads = lax.scan(
        spread_grads, start_query, (key_blocks, value_blocks, keep_blocks)
    )
    total_rows = key_heads.shape[0]
    model_width = head_count * query_heads.shape[2]
    grad_key_all = block_grads[0].reshape(total_rows, model_width)
    grad_value_all = block_grads[1].reshape(total_rows, model_width)
    return (grad_query * score_scale, grad_key_all, grad_value_all)


def column_sum(matrix_low):
    return jnp.sum(matrix_low.astype(jnp.float32), axis=0)


def body(
    tokens_in,
    lengths,
    ln1_gain,
    ln1_bias,
    w_qkv,
    bias_query,
    bias_value,
    w_out,
    bias_out,
    ln2_gain,
    ln2_bias,
    w_up,
    bias_up,
    w_down,
    bias_down,
    proj_patch,
    proj_class,
    class_emb,
    d_masks,
):
    row_count, model_width = tokens_in.shape
    head_size = HEAD_DIM
    head_count = model_width // head_size
    seq_devices = lax.axis_size("seq")
    grp_devices = lax.axis_size("grp")
    seq_total = row_count * seq_devices
    key_span = min(512, seq_total)
    score_scale = head_size ** (-0.5)
    mask_scale = math.sqrt(model_width)
    length_here = lengths[0]
    first_row = lax.axis_index("seq") * row_count
    valid_rows = (first_row + jnp.arange(row_count, dtype=jnp.int32) < length_here).astype(
        jnp.float32
    )
    key_keep = jnp.arange(seq_total, dtype=jnp.int32) < length_here
    tokens = tokens_in.astype(jnp.float32)
    normed_one, norm_one_back = jax.vjp(layer_norm, tokens, ln1_gain, ln1_bias)
    normed_low = normed_one.astype(jnp.bfloat16)
    zero_keys = jnp.zeros_like(bias_query)
    mixed = jnp.dot(normed_low, w_qkv, preferred_element_type=jnp.float32)
    mixed = mixed + jnp.concatenate([bias_query, zero_keys, bias_value])
    mixed_low = mixed.astype(jnp.bfloat16)
    query_heads = mixed_low[:, :model_width].reshape(row_count, head_count, head_size)
    key_rows = mixed_low[:, model_width : 2 * model_width]
    value_rows = mixed_low[:, 2 * model_width :]
    key_all, value_all = (
        lax.all_gather(key_rows, "seq", axis=0, tiled=True),
        lax.all_gather(value_rows, "seq", axis=0, tiled=True),
    )
    key_heads = key_all.reshape(seq_total, head_count, head_size)
    value_heads = value_all.reshape(seq_total, head_count, head_size)
    attended, log_mass = attend_forward(
        query_heads, key_heads, value_heads, key_keep, score_scale, key_span
    )
    attended_low = attended.reshape(row_count, model_width).astype(jnp.bfloat16)
    branch = jnp.dot(attended_low, w_out, preferred_element_type=jnp.float32) + bias_out
    middle = tokens + branch
    normed_two, norm_two_back = jax.vjp(layer_norm, middle, ln2_gain, ln2_bias)
    normed_two_low = normed_two.astype(jnp.bfloat16)
    hidden = jnp.dot(normed_two_low, w_up, preferred_element_type=jnp.float32) + bias_up
    active, gelu_back = jax.vjp(gelu_exact, hidden)
    active_low = active.astype(jnp.bfloat16)
    final = middle + (jnp.dot(active_low, w_down, preferred_element_type=jnp.float32) + bias_down)
    final_low = final.astype(jnp.bfloat16)
    patches = jnp.dot(final_low, proj_patch, preferred_element_type=jnp.float32)
    patch_unit, patch_back = jax.vjp(unit_rows, patches)
    patch_low = patch_unit.astype(jnp.bfloat16)
    classes = jnp.dot(class_emb, proj_class, preferred_element_type=jnp.float32)
    class_unit, class_back = jax.vjp(unit_rows, classes)
    class_low = class_unit.astype(jnp.bfloat16)
    mask_out = jnp.einsum("rd,cd->rc", patch_low, class_low, preferred_element_type=jnp.float32)
    mask_out = (mask_out * mask_scale * valid_rows[:, None]).astype(jnp.bfloat16)
    mask_grad = (d_masks.astype(jnp.float32) * valid_rows[:, None]).astype(jnp.bfloat16)
    grad_patch_unit = jnp.dot(mask_grad, class_low, preferred_element_type=jnp.float32) * mask_scale
    class_part = (
        jnp.einsum("rc,rd->cd", mask_grad, patch_low, preferred_element_type=jnp.float32)
        * mask_scale
    )
    class_total = lax.psum(class_part, ("grp", "seq"))
    grad_classes = class_back(class_total)[0].astype(jnp.bfloat16)
    class_proj_full = jnp.einsum(
        "cd,ce->de", class_emb, grad_classes, preferred_element_type=jnp.float32
    )
    class_emb_full = jnp.einsum(
        "ce,de->cd", grad_classes, proj_class, preferred_element_type=jnp.float32
    )
    grad_patches = patch_back(grad_patch_unit)[0].astype(jnp.bfloat16)
    grad_proj_patch = jnp.einsum(
        "rd,re->de", final_low, grad_patches, preferred_element_type=jnp.float32
    )
    grad_final = jnp.einsum(
        "re,de->rd", grad_patches, proj_patch, preferred_element_type=jnp.float32
    )
    grad_feed = grad_final.astype(jnp.bfloat16)
    grad_w_down = jnp.einsum("rf,rd->fd", active_low, grad_feed, preferred_element_type=jnp.float32)
    grad_bias_down = column_sum(grad_feed)
    grad_active = jnp.einsum("rd,fd->rf", grad_feed, w_down, preferred_element_type=jnp.float32)
    grad_hidden = gelu_back(grad_active)[0].astype(jnp.bfloat16)
    grad_w_up = jnp.einsum(
        "rd,rf->df", normed_two_low, grad_hidden, preferred_element_type=jnp.float32
    )
    grad_bias_up = column_sum(grad_hidden)
    grad_normed_two = jnp.einsum("rf,df->rd", grad_hidden, w_up, preferred_element_type=jnp.float32)
    grad_middle_norm, grad_ln2_gain, grad_ln2_bias = norm_two_back(grad_normed_two)
    grad_middle = grad_final + grad_middle_norm
    grad_branch = grad_middle.astype(jnp.bfloat16)
    grad_w_out = jnp.einsum(
        "rd,re->de", attended_low, grad_branch, preferred_element_type=jnp.float32
    )
    grad_bias_out = column_sum(grad_branch)
    grad_attended = jnp.einsum("re,de->rd", grad_branch, w_out, preferred_element_type=jnp.float32)
    grad_heads = grad_attended.astype(jnp.bfloat16).reshape(row_count, head_count, head_size)
    grad_query, grad_key_all, grad_value_all = attend_backward(
        query_heads,
        key_heads,
        value_heads,
        key_keep,
        grad_heads,
        log_mass,
        attended,
        score_scale,
        key_span,
    )
    grad_key_own, grad_value_own = (
        lax.psum_scatter(
            grad_key_all.astype(jnp.bfloat16), "seq", scatter_dimension=0, tiled=True
        ).astype(jnp.float32),
        lax.psum_scatter(
            grad_value_all.astype(jnp.bfloat16), "seq", scatter_dimension=0, tiled=True
        ).astype(jnp.float32),
    )
    grad_mixed = jnp.concatenate(
        [grad_query.reshape(row_count, model_width), grad_key_own, grad_value_own], axis=1
    ).astype(jnp.bfloat16)
    grad_w_qkv = jnp.einsum("rd,rm->dm", normed_low, grad_mixed, preferred_element_type=jnp.float32)
    grad_bias_all = column_sum(grad_mixed)
    grad_bias_query = grad_bias_all[:model_width]
    grad_bias_value = grad_bias_all[2 * model_width :]
    grad_normed_one = jnp.einsum("rm,dm->rd", grad_mixed, w_qkv, preferred_element_type=jnp.float32)
    grad_tokens_norm, grad_ln1_gain, grad_ln1_bias = norm_one_back(grad_normed_one)
    grad_tokens = (grad_middle + grad_tokens_norm).astype(jnp.bfloat16)
    row_parts = (
        lax.psum_scatter(grad_w_qkv, "grp", scatter_dimension=0, tiled=True),
        lax.psum_scatter(grad_w_out, "grp", scatter_dimension=0, tiled=True),
        lax.psum_scatter(grad_w_up, "grp", scatter_dimension=0, tiled=True),
        lax.psum_scatter(grad_w_down, "grp", scatter_dimension=0, tiled=True),
        lax.psum_scatter(grad_proj_patch, "grp", scatter_dimension=0, tiled=True),
        lax.psum_scatter(grad_ln1_gain, "grp", scatter_dimension=0, tiled=True),
        lax.psum_scatter(grad_ln1_bias, "grp", scatter_dimension=0, tiled=True),
        lax.psum_scatter(grad_bias_query, "grp", scatter_dimension=0, tiled=True),
        lax.psum_scatter(grad_bias_value, "grp", scatter_dimension=0, tiled=True),
        lax.psum_scatter(grad_bias_out, "grp", scatter_dimension=0, tiled=True),
        lax.psum_scatter(grad_ln2_gain, "grp", scatter_dimension=0, tiled=True),
        lax.psum_scatter(grad_ln2_bias, "grp", scatter_dimension=0, tiled=True),
        lax.psum_scatter(grad_bias_up, "grp", scatter_dimension=0, tiled=True),
        lax.psum_scatter(grad_bias_down, "grp", scatter_dimension=0, tiled=True),
    )
    matrix_parts = (
        lax.psum_scatter(
            row_parts[0].astype(jnp.bfloat16), "seq", scatter_dimension=1, tiled=True
        ).astype(jnp.float32),
        lax.psum_scatter(
            row_parts[1].astype(jnp.bfloat16), "seq", scatter_dimension=1, tiled=True
        ).astype(jnp.float32),
        lax.psum_scatter(
            row_parts[2].astype(jnp.bfloat16), "seq", scatter_dimension=1, tiled=True
        ).astype(jnp.float32),
        lax.psum_scatter(
            row_parts[3].astype(jnp.bfloat16), "seq", scatter_dimension=1, tiled=True
        ).astype(jnp.float32),
        lax.psum_scatter(
            row_parts[4].astype(jnp.bfloat16), "seq", scatter_dimension=1, tiled=True
        ).astype(jnp.float32),
    )
    vector_parts = lax.psum(
        (
            row_parts[5],
            row_parts[6],
            row_parts[7],
            row_parts[8],
            row_parts[9],
            row_parts[10],
            row_parts[11],
            row_parts[12],
            row_parts[13],
        ),
        "seq",
    )
    rows_each = model_width // grp_devices
    cols_each = model_width // seq_devices
    grp_here = lax.axis_index("grp")
    seq_here = lax.axis_index("seq")
    grad_proj_class = lax.dynamic_slice(
        class_proj_full, (grp_here * rows_each, seq_here * cols_each), (rows_each, cols_each)
    )
    grad_class_emb = lax.dynamic_slice_in_dim(class_emb_full, grp_here * rows_each, rows_each, 1)
    return (
        mask_out,
        grad_tokens,
        vector_parts[0],
        vector_parts[1],
        matrix_parts[0],
        vector_parts[2],
        vector_parts[3],
        matrix_parts[1],
        vector_parts[4],
        vector_parts[5],
        vector_parts[6],
        matrix_parts[2],
        vector_parts[7],
        matrix_parts[3],
        vector_parts[8],
        matrix_parts[4],
        grad_proj_class,
        grad_class_emb,
    )


def solution(mesh):
    return jax.shard_map(
        body,
        mesh=mesh,
        in_specs=(
            P(("grp", "seq"), None),
            P("grp"),
            P(),
            P(),
            P(),
            P(),
            P(),
            P(),
            P(),
            P(),
            P(),
            P(),
            P(),
            P(),
            P(),
            P(),
            P(),
            P(),
            P(("grp", "seq"), None),
        ),
        out_specs=(
            P(("grp", "seq"), None),
            P(("grp", "seq"), None),
            P("grp"),
            P("grp"),
            P("grp", "seq"),
            P("grp"),
            P("grp"),
            P("grp", "seq"),
            P("grp"),
            P("grp"),
            P("grp"),
            P("grp", "seq"),
            P("grp"),
            P("grp", "seq"),
            P("grp"),
            P("grp", "seq"),
            P("grp", "seq"),
            P(None, "grp"),
        ),
        check_vma=False,
    )
```

profile of v0, /device:TPU:0, one launch (start us, length us, event | category | flops | bytes accessed | tf_op | source)
XLA Modules:
  0.0 1562.3 jit_solution(7666178320111044407)
XLA Ops:
  30.2 29.2 %all-gather.5.cloned.1.call-done = bf16[3072,768]{1,0:T(8,128)(2,1)} async-done(((bf16[768,768]{1,0:T(8,128)(2,1)}), bf16[3072,768]{1,0:T(8,128)(2,1)}) %all-gather.5.cloned.1.call-update) | async-done | bytes 4718608 | tf_op jit(solution)/shard_map/all_gather | solution.py:186
  59.4 15.0 reshape.189
  74.4 13.5 copy.80
  88.0 165.2 %while.39 = (s32[]{:T(128)}, f32[12,768]{1,0:T(8,128)}, f32[12,768]{1,0:T(8,128)}, pred[6,512]{1,0:T(8,128)(4,1)S(1)}, bf16[6,512,12,64]{1,3,2,0:T(8,128)(2,1)},...) while((s32[]{:T(128)}, f32[12,768]{1,0:T(8,128)}, f32[12,768]{1,0:T(8,128)}, ...), condition=%wide.region_5.6_spmd.clone, body=%wide.region_2.5_spmd.clone.sunk | while | flops 637056000 | bytes 40196704 | solution.py:68
  88.0 12.4 bitcast_reduce_fusion.2
  101.8 10.8 fusion.145
  115.5 12.3 bitcast_reduce_fusion.2
  129.3 10.8 fusion.145
  143.0 12.3 bitcast_reduce_fusion.2
  156.8 10.8 fusion.145
  170.6 12.3 bitcast_reduce_fusion.2
  184.3 10.8 fusion.145
  198.1 12.3 bitcast_reduce_fusion.2
  211.9 10.8 fusion.145
  225.6 12.3 bitcast_reduce_fusion.2
  239.4 10.8 fusion.145
  253.2 15.0 reshape.188
  268.1 13.6 copy.79
  283.2 61.1 %while.40 = (s32[]{:T(128)}, f32[768,12,64]{0,2,1:T(8,128)}, bf16[6,512,12,64]{1,3,2,0:T(8,128)(2,1)}, pred[6,512]{1,0:T(8,128)(4,1)S(1)}, bf16[6,512,12,64]{1,3...) while((s32[]{:T(128)}, f32[768,12,64]{0,2,1:T(8,128)}, ...), condition=%wide.region_7.8_spmd.clone, body=%wide.region_6.7_spmd.clone.sunk | while | flops 1228013568 | bytes 7522923 | solution.py:81
  283.4 9.5 bitcast_add_fusion.4
  292.9 10.2 bitcast_add_fusion.4
  303.2 10.2 bitcast_add_fusion.4
  313.5 10.2 bitcast_add_fusion.4
  323.7 10.2 bitcast_add_fusion.4
  334.0 10.2 bitcast_add_fusion.4
  350.3 28.6 %multiply_convert_fusion.1 = (bf16[768,3072]{1,0:T(8,128)(2,1)S(1)}, f32[768,3072]{1,0:T(8,128)}, f32[768,3072]{1,0:T(8,128)}) fusion(f32[3072]{0:T(1024)S(1)} %copy-done.54, bf16[768,3072]{1,0:T(8,128)(2,1)S(1)} %bitcast.171, f32[768,768]{0,1:T(8,128)S(1)} %get-tuple-element.449, f32[768]{0:T(1024)S(1)} %copy-done.57, f32[768]{0:T(1024)S(1)} %copy-done.42, ...), kind=kOutput, calls=%fused_computation.51 | convolution fusion | flops 3782541312 | bytes 30695424 | tf_op jit(solution)/shard_map/dot_general | solution.py:199
  395.1 13.0 convert_reduce_fusion
  408.1 9.9 fusion.86
  433.8 291.4 %while.41 = (s32[]{:T(128)}, f32[768,12,64]{0,2,1:T(8,128)}, bf16[6,512,12,64]{1,3,2,0:T(8,128)(2,1)}, bf16[6,512,12,64]{1,3,2,0:T(8,128)(2,1)}, bf16[6,512,12,6...) while((s32[]{:T(128)}, f32[768,12,64]{0,2,1:T(8,128)}, ...), condition=%wide.region_16.17_spmd.clone, body=%wide.region_15.16_spmd.clone.sunk | while | flops 3068657664 | bytes 142766832 | solution.py:125
  434.4 10.6 fusion.160
  445.0 10.9 multiply_convert_fusion.13
  463.5 7.0 bitcast_add_fusion.5
  470.6 11.9 bitcast_dynamic-update-slice_fusion.5
  482.5 10.6 fusion.160
  493.2 10.8 multiply_convert_fusion.13
  511.5 7.7 bitcast_add_fusion.5
  519.3 11.9 bitcast_dynamic-update-slice_fusion.5
  531.2 10.6 fusion.160
  541.8 10.7 multiply_convert_fusion.13
  560.1 7.7 bitcast_add_fusion.5
  567.8 11.9 bitcast_dynamic-update-slice_fusion.5
  579.7 10.6 fusion.160
  590.4 10.7 multiply_convert_fusion.13
  608.6 7.7 bitcast_add_fusion.5
  616.3 11.9 bitcast_dynamic-update-slice_fusion.5
  628.2 10.6 fusion.160
  638.8 10.7 multiply_convert_fusion.13
  657.1 7.7 bitcast_add_fusion.5
  664.8 11.9 bitcast_dynamic-update-slice_fusion.5
  676.7 10.6 fusion.160
  687.4 10.7 multiply_convert_fusion.13
  705.6 7.7 bitcast_add_fusion.5
  713.3 11.8 bitcast_dynamic-update-slice_fusion.5
  751.4 10.7 fusion.67
  769.3 10.7 fusion.77
  784.4 50.4 %reduce-scatter.23.cloned.1.call-done = bf16[768,768]{0,1:T(8,128)(2,1)} async-done(((bf16[3072,768]{0,1:T(8,128)(2,1)}), bf16[768,768]{0,1:T(8,128)(2,1)}) %reduce-scatter.23.cloned.1.call-update) | async-done | bytes 1179664 | tf_op jit(solution)/shard_map/reduce_scatter | solution.py:267
  834.9 8.4 fusion.73
  848.8 117.9 %all-reduce.13.cloned.1.call-done = f32[150,768]{1,0:T(8,128)} async-done(((f32[150,768]{1,0:T(8,128)}), f32[150,768]{1,0:T(8,128)}) %all-reduce.13.cloned.1.call-update) | async-done | bytes 460816 | tf_op jit(solution)/shard_map/psum | solution.py:218
  968.6 165.9 %reduce-scatter.33.cloned.1.call-done = f32[384,768]{1,0:T(8,128)} async-done(((f32[3072,768]{1,0:T(8,128)}), f32[384,768]{1,0:T(8,128)}) %reduce-scatter.33.cloned.1.call-update) | async-done | bytes 1179664 | tf_op jit(solution)/shard_map/reduce_scatter | solution.py:285
  1148.1 8.5 reduce-scatter.43.cloned.1.call-done
  1159.5 19.8 %reduce-scatter.39.cloned.1.call-done = bf16[192,96]{1,0:T(8,128)(2,1)} async-done(((bf16[768,96]{1,0:T(8,128)(2,1)}), bf16[192,96]{1,0:T(8,128)(2,1)}) %reduce-scatter.39.cloned.1.call-update) | async-done | bytes 36880
  1182.3 164.4 %reduce-scatter.29.cloned.1.call-done = f32[96,3072]{1,0:T(8,128)} async-done(((f32[768,3072]{1,0:T(8,128)}), f32[96,3072]{1,0:T(8,128)}) %reduce-scatter.29.cloned.1.call-update) | async-done | bytes 1179664 | tf_op jit(solution)/shard_map/reduce_scatter | solution.py:284
  1366.0 112.8 %reduce-scatter.25.cloned.1.call-done = f32[96,2304]{1,0:T(8,128)} async-done(((f32[768,2304]{1,0:T(8,128)}), f32[96,2304]{1,0:T(8,128)}) %reduce-scatter.25.cloned.1.call-update) | async-done | bytes 884752 | tf_op jit(solution)/shard_map/reduce_scatter | solution.py:282
  1484.2 36.8 %all-reduce.9 = (f32[768]{0:T(1024)}, f32[768]{0:T(1024)}, f32[768]{0:T(1024)}, f32[768]{0:T(1024)}, f32[768]{0:T(1024)}, /*index=5*/f32[768]{0:T(1024)}, f32[768]{0:T(1024)}, f32[3072]{0:T(1024)}, f32[768]{0:T(1024)}) all-reduce(f32[768]{0:T(1024)} %get-tuple-element.362, ...), channel_id=4, replica_groups=mesh['grp'=8,'seq'=4] {'grp'}, use_global_device_ids=true, to_apply=%region_22.23.clone | all-reduce | flops 9216 | bytes 73728
  (349 shorter events, 255.3 us)
Async XLA Ops:
  7.2 6.5 copy-start
  7.2 6.4 copy-start.47
  7.2 6.4 copy-start.46
  7.2 6.4 copy-start.35
  7.2 6.4 copy-start.58
  7.2 52.1 %all-gather.5.cloned.1.call-start = ((), (), s32[]{:S(2)}) async-start(), calls=%async_computation.13 | async-start | bytes 5898240 | tf_op jit(solution)/shard_map/all_gather | solution.py:186
  9.8 3.9 copy-start.3
  11.4 5.8 copy-start.22
  13.1 4.1 copy-start.31
  19.1 234.1 %all-gather.3.cloned.1.call-start = ((), (), s32[]{:S(2)}) async-start(), calls=%async_computation.12 | async-start | bytes 5898240 | tf_op jit(solution)/shard_map/all_gather | solution.py:187
  19.8 742.3 %reduce-scatter.35.cloned.1.call-start = ((), (), s32[]{:S(2)}) async-start(), calls=%async_computation.21 | async-start | bytes 2654208 | tf_op jit(solution)/shard_map/reduce_scatter | solution.py:286
  26.3 48.1 %copy-start.40 = (f32[150]{0:T(256)}, f32[150]{0:T(256)S(1)}, u32[]{:S(2)}) copy-start(f32[150]{0:T(256)S(1)} %add_rsqrt_fusion.1) | copy-start | bytes 1804
  346.6 32.3 %slice-start = ((s8[4718592]{0:T(1024)(128)(4,1)}), s8[4194304]{0:T(1024)(128)(4,1)S(1)}, s32[]{:S(2)}) async-start(s8[4718592]{0:T(1024)(128)(4,1)} %bitcast.168), calls=%async_computation.27 | async-start | bytes 8388608
  347.9 31.0 %copy-start.7 = (f32[768,768]{0,1:T(8,128)}, f32[768,768]{0,1:T(8,128)S(1)}, u32[]{:S(2)}) copy-start(f32[768,768]{0,1:T(8,128)S(1)} %get-tuple-element.449) | copy-start | bytes 7077892
  348.0 77.0 %copy-start.24 = (f32[768]{0:T(1024)}, f32[768]{0:T(1024)S(1)}, u32[]{:S(2)}) copy-start(f32[768]{0:T(1024)S(1)} %broadcast_multiply_fusion.1) | copy-start | bytes 9220
  350.3 74.7 %copy-start.38 = (f32[768]{0:T(1024)}, f32[768]{0:T(1024)S(1)}, u32[]{:S(2)}) copy-start(f32[768]{0:T(1024)S(1)} %fusion.66) | copy-start | bytes 9220
  350.3 28.7 %slice-start.1 = ((s8[4718592]{0:T(1024)(128)(4,1)}), s8[524288]{0:T(1024)(128)(4,1)S(1)}, s32[]{:S(2)}) async-start(s8[4718592]{0:T(1024)(128)(4,1)} %bitcast.168), calls=%async_computation.28 | async-start | bytes 1048576
  350.3 28.7 %copy-start.56 = (f32[768]{0:T(1024)S(1)}, f32[768]{0:T(1024)}, u32[]{:S(2)}) copy-start(f32[768]{0:T(1024)} %param.39) | copy-start | bytes 9220
  378.9 4.2 copy-start.59
  379.0 4.1 copy-start.13
  379.0 4.1 copy-start.51
  391.7 373.9 %reduce-scatter.27.cloned.1.call-start = ((), (), s32[]{:S(2)}) async-start(), calls=%async_computation.17 | async-start | bytes 2654208 | tf_op jit(solution)/shard_map/reduce_scatter | solution.py:283
  408.1 9.9 copy-start.60
  421.1 3.9 copy-start.8
  421.1 3.9 copy-start.9
  421.1 3.9 copy-start.43
  433.8 350.6 %reduce-scatter.21.cloned.1.call-start = ((), (), s32[]{:S(2)}) async-start(), calls=%async_computation.14 | async-start | bytes 5898240 | tf_op jit(solution)/shard_map/reduce_scatter | solution.py:264
  434.3 10.7 copy-start.26
  434.3 10.7 copy-start.27
  445.0 14.6 copy-start.2
  482.5 10.7 copy-start.26
  482.5 10.7 copy-start.27
  493.2 14.6 copy-start.2
  504.0 3.7 copy-start.1
  531.2 10.7 copy-start.26
  531.2 10.7 copy-start.27
  541.8 14.4 copy-start.2
  552.5 3.7 copy-start.1
  579.7 10.7 copy-start.26
  579.7 10.7 copy-start.27
  590.4 14.4 copy-start.2
  628.2 10.7 copy-start.26
  628.2 10.7 copy-start.27
  638.8 14.4 copy-start.2
  676.7 10.7 copy-start.26
  676.7 10.7 copy-start.27
  687.3 14.4 copy-start.2
  736.2 98.6 %reduce-scatter.23.cloned.1.call-start = ((), (), s32[]{:S(2)}) async-start(), calls=%async_computation.15 | async-start | bytes 5898240 | tf_op jit(solution)/shard_map/reduce_scatter | solution.py:267
  747.4 219.3 %all-reduce.13.cloned.1.call-start = ((), (), s32[]{:S(2)}) async-start(), calls=%async_computation.22 | async-start | bytes 933888 | tf_op jit(solution)/shard_map/psum | solution.py:218
  751.3 383.2 %reduce-scatter.33.cloned.1.call-start = ((), (), s32[]{:S(2)}) async-start(), calls=%async_computation.20 | async-start | bytes 10616832 | tf_op jit(solution)/shard_map/reduce_scatter | solution.py:285
  762.0 7.2 copy-start.25
  762.0 7.2 copy-start.39
  762.0 7.2 copy-start.44
  762.0 394.5 %reduce-scatter.43.cloned.1.call-start = ((), (), s32[]{:S(2)}) async-start(), calls=%async_computation.26 | async-start | bytes 245760
  765.5 413.8 %reduce-scatter.39.cloned.1.call-start = ((), (), s32[]{:S(2)}) async-start(), calls=%async_computation.24 | async-start | bytes 245760
  769.0 577.7 %reduce-scatter.29.cloned.1.call-start = ((), (), s32[]{:S(2)}) async-start(), calls=%async_computation.18 | async-start | bytes 10616832 | tf_op jit(solution)/shard_map/reduce_scatter | solution.py:284
  780.0 54.9 %copy-start.23 = (f32[768]{0:T(1024)S(1)}, f32[768]{0:T(1024)}, u32[]{:S(2)}) copy-start(f32[768]{0:T(1024)} %copy-done.22) | copy-start | bytes 9220
  780.0 54.9 %copy-start.32 = (f32[768]{0:T(1024)S(1)}, f32[768]{0:T(1024)}, u32[]{:S(2)}) copy-start(f32[768]{0:T(1024)} %copy-done.31) | copy-start | bytes 9220
  780.0 54.8 %copy-start.36 = (f32[768]{0:T(1024)S(1)}, f32[768]{0:T(1024)}, u32[]{:S(2)}) copy-start(f32[768]{0:T(1024)} %param.27) | copy-start | bytes 9220
  780.0 698.8 %reduce-scatter.25.cloned.1.call-start = ((), (), s32[]{:S(2)}) async-start(), calls=%async_computation.16 | async-start | bytes 7962624 | tf_op jit(solution)/shard_map/reduce_scatter | solution.py:282
  843.3 703.6 %reduce-scatter.41.cloned.1.call-start = ((), (), s32[]{:S(2)}) async-start(), calls=%async_computation.25 | async-start | bytes 737280
  848.8 290.7 %copy-start.41 = (f32[150]{0:T(256)S(1)}, f32[150]{0:T(256)}, u32[]{:S(2)}) copy-start(f32[150]{0:T(256)} %copy-done.40) | copy-start | bytes 1804
  1138.8 411.6 %reduce-scatter.31.cloned.1.call-start = ((), (), s32[]{:S(2)}) async-start(), calls=%async_computation.19 | async-start | bytes 737280 | tf_op jit(solution)/shard_map/reduce_scatter | solution.py:304
  1348.8 203.2 %reduce-scatter.37.cloned.1.call-start = ((), (), s32[]{:S(2)}) async-start(), calls=%async_computation.23 | async-start | bytes 737280
  (36 other events, 78.2 us)
Sparse Core Ops, SparseCore 0:
  19.2 40.1 all-gather.4
  60.9 37.4 all-gather.2
  391.8 69.2 reduce-scatter.34
  464.4 67.9 reduce-scatter.26
  736.4 48.0 reduce-scatter.20
  787.0 47.7 reduce-scatter.22
  840.2 126.5 all-reduce.12
  970.7 163.7 reduce-scatter.32
  1137.7 18.8 reduce-scatter.42
  1159.5 19.7 reduce-scatter.38
  1183.3 163.2 reduce-scatter.28
  1350.7 128.1 reduce-scatter.24
  1481.3 21.1 reduce-scatter.40
  1504.8 22.0 reduce-scatter.30
  1529.3 22.0 reduce-scatter.36
where the time goes:
time: 1570 us; the launch traced here: 1560 us
  waiting for transfers between devices  671 us (43%)
  matrix products  526 us (34%)
  local copies, waits for them, and re-layouts  171 us (11%)
  other arithmetic  131 us (8%)
  blocking collectives  43.3 us (3%)
  between operations  17.1 us (1%)
    reduce_scatter x1, waiting for transfers between devices, body(): lax.psum_scatter(grad_w_down, 'grp', scatter_dimension=0, tiled=True)  166 us
    reduce_scatter x1, waiting for transfers between devices, body(): lax.psum_scatter(grad_w_up, 'grp', scatter_dimension=0, tiled=True)  164 us
    dot_general x12, matrix products, score_block(): jnp.einsum('qhd,khd->hqk', query_heads, key_block, preferred_element_type...  138 us
    psum x1, waiting for transfers between devices, body(): class_total = lax.psum(class_part, ('grp', 'seq'))  118 us
    reduce_scatter x1, waiting for transfers between devices, body(): lax.psum_scatter(grad_w_qkv, 'grp', scatter_dimension=0, tiled=True)  113 us
    unnamed x148, local copies, waits for them, and re-layouts  81.5 us
    dot_general x6, matrix products, spread_grads(): jnp.einsum('hqk,qhd->khd', prob_rows.astype(jnp.bfloat16), grad_heads, pr...  71.3 us
    reduce_sum x6, other arithmetic, gather_stats(): jnp.sum(jnp.exp(scores - new_top[..., None]), axis=-1)  64.9 us
  transfers between devices with their start and end apart: 15, of which 9 were waited for; matrix products, arithmetic and copies ran while one was open for 41% of the time, Pallas kernels for 0%

commit v1 on v0

v1 whole, which is shorter than its diff:
```python
import functools
import math

import jax
import jax.numpy as jnp
from jax import lax
from jax.experimental import pallas as pl
from jax.experimental.pallas import tpu as pltpu
from jax.sharding import PartitionSpec as P

HEAD_DIM = 64
LANES = 128
EPS_NORM = 1e-06
EPS_UNIT = 1e-06
NEG_FILL = -1e30
LOG2E = math.log2(math.e)
F32 = jnp.float32
BF16 = jnp.bfloat16
MIB = 1 << 20


def dot_nn(a, b):
    return lax.dot_general(a, b, (((1,), (0,)), ((), ())), preferred_element_type=F32)


def dot_nt(a, b):
    return lax.dot_general(a, b, (((1,), (1,)), ((), ())), preferred_element_type=F32)


def dot_tn(a, b):
    return lax.dot_general(a, b, (((0,), (0,)), ((), ())), preferred_element_type=F32)


def attend_forward_kernel(q_ref, k_ref, v_ref, out_ref, mass_ref):
    scores = dot_nt(k_ref[...], q_ref[...])
    top = jnp.max(scores, axis=0, keepdims=True)
    prob = jnp.exp2((scores - top) * LOG2E).astype(BF16)
    summed = dot_tn(v_ref[...], prob)
    total = summed[HEAD_DIM : HEAD_DIM + 1]
    out_ref[...] = (summed[:HEAD_DIM] / total).astype(BF16)
    mass_ref[0] = top * LOG2E + jnp.log2(total)


def attend_forward(queries, keys, values):
    rows, width = queries.shape
    span = keys.shape[0]
    heads = width // LANES
    tile = rows // 2
    return pl.pallas_call(
        attend_forward_kernel,
        grid=(heads, 2),
        in_specs=[
            pl.BlockSpec((tile, LANES), lambda h, i: (i, h)),
            pl.BlockSpec((span, LANES), lambda h, i: (0, h)),
            pl.BlockSpec((span, LANES), lambda h, i: (0, h)),
        ],
        out_specs=[
            pl.BlockSpec((HEAD_DIM, tile), lambda h, i: (h, i)),
            pl.BlockSpec((1, 1, tile), lambda h, i: (h, 0, i)),
        ],
        out_shape=[
            jax.ShapeDtypeStruct((heads * HEAD_DIM, rows), BF16),
            jax.ShapeDtypeStruct((heads, 1, rows), F32),
        ],
        compiler_params=pltpu.CompilerParams(vmem_limit_bytes=50 * MIB),
        cost_estimate=pl.CostEstimate(
            flops=8 * heads * rows * span * LANES,
            bytes_accessed=(rows + 2 * span) * width * 2,
            transcendentals=heads * rows * span,
        ),
        name="attend_forward",
    )(queries, keys, values)


def attend_backward_kernel(
    q_ref,
    gout_ref,
    out_ref,
    mass_ref,
    k_ref,
    v_ref,
    gq_ref,
    gkv_ref,
    q_t,
    q_clean,
    gout_t,
    delta,
    gq_sum,
):
    step = pl.program_id(1)

    @pl.when(step == 0)
    def _():
        q_now = q_ref[...]
        column = lax.broadcasted_iota(jnp.int32, q_now.shape, 1)
        q_t[...] = q_now.T
        q_clean[...] = jnp.where(column < HEAD_DIM, jnp.zeros_like(q_now), q_now)
        turned = gout_ref[...].T
        gout_t[...] = turned
        delta[...] = jnp.sum(
            turned[:HEAD_DIM].astype(F32) * out_ref[...].astype(F32), axis=0, keepdims=True
        )

    key_now = k_ref[...]
    scores = dot_nn(key_now, q_t[...])
    prob = jnp.exp2(scores * LOG2E - mass_ref[0])
    gprob = dot_nn(v_ref[...], gout_t[...])
    gscore = (prob * (gprob - delta[...])).astype(BF16)
    gkv_ref[...] = (
        dot_nn(prob.astype(BF16), gout_ref[...]) + dot_nn(gscore, q_clean[...])
    ).astype(BF16)
    part = dot_tn(key_now, gscore)

    @pl.when(step == 0)
    def _():
        gq_sum[...] = part

    @pl.when(step > 0)
    def _():
        gq_sum[...] += part

    @pl.when(step == pl.num_programs(1) - 1)
    def _():
        gq_ref[...] = (gq_sum[HEAD_DIM:] * HEAD_DIM**-0.5).astype(BF16)


def attend_backward(queries, gouts, outs_t, mass, keys, values):
    rows, width = queries.shape
    span = keys.shape[0]
    heads = width // LANES
    tile = min(1024, span)
    return pl.pallas_call(
        attend_backward_kernel,
        grid=(heads, span // tile),
        in_specs=[
            pl.BlockSpec((rows, LANES), lambda h, j: (0, h)),
            pl.BlockSpec((rows, LANES), lambda h, j: (0, h)),
            pl.BlockSpec((HEAD_DIM, rows), lambda h, j: (h, 0)),
            pl.BlockSpec((1, 1, rows), lambda h, j: (h, 0, 0)),
            pl.BlockSpec((tile, LANES), lambda h, j: (j, h)),
            pl.BlockSpec((tile, LANES), lambda h, j: (j, h)),
        ],
        out_specs=[
            pl.BlockSpec((HEAD_DIM, rows), lambda h, j: (h, 0)),
            pl.BlockSpec((tile, LANES), lambda h, j: (j, h)),
        ],
        out_shape=[
            jax.ShapeDtypeStruct((heads * HEAD_DIM, rows), BF16),
            jax.ShapeDtypeStruct((span, width), BF16),
        ],
        scratch_shapes=[
            pltpu.VMEM((LANES, rows), BF16),
            pltpu.VMEM((rows, LANES), BF16),
            pltpu.VMEM((LANES, rows), BF16),
            pltpu.VMEM((1, rows), F32),
            pltpu.VMEM((LANES, rows), F32),
        ],
        compiler_params=pltpu.CompilerParams(vmem_limit_bytes=56 * MIB),
        cost_estimate=pl.CostEstimate(
            flops=20 * heads * rows * span * LANES,
            bytes_accessed=(2 * rows + 3 * span) * width * 2,
            transcendentals=heads * rows * span,
        ),
        name="attend_backward",
    )(queries, gouts, outs_t, mass, keys, values)


def layer_norm(matrix_rows, gain_vec, shift_vec):
    row_mean = jnp.mean(matrix_rows, axis=-1, keepdims=True)
    centred = matrix_rows - row_mean
    row_var = jnp.mean(centred * centred, axis=-1, keepdims=True)
    return centred * lax.rsqrt(row_var + EPS_NORM) * gain_vec + shift_vec


def unit_rows(matrix_rows):
    return matrix_rows * lax.rsqrt(
        jnp.sum(matrix_rows * matrix_rows, axis=-1, keepdims=True) + EPS_UNIT
    )


def gelu_exact(values_in):
    return jax.nn.gelu(values_in, approximate=False)


def column_sum(matrix_low):
    return jnp.sum(matrix_low.astype(F32), axis=0)


def swap(value, axis, bit):
    size = lax.axis_size(axis)
    return lax.ppermute(value, axis, [(i, i ^ bit) for i in range(size)])


def row_steps(part, names):
    groups = lax.axis_size("grp")
    bits = groups.bit_length() - 1
    here = lax.axis_index("grp")
    for name in names:
        axis = bits - 1 - name
        mine = (here >> name) & 1
        send = lax.dynamic_index_in_dim(part, 1 - mine, axis, keepdims=True)
        keep = lax.dynamic_index_in_dim(part, mine, axis, keepdims=True)
        got = swap(send, "grp", 1 << name)
        part = (keep.astype(F32) + got.astype(F32)).astype(BF16)
    return part


def split_rows(part):
    groups = lax.axis_size("grp")
    bits = groups.bit_length() - 1
    return part.reshape((2,) * bits + (part.shape[0] // groups, part.shape[1]))


def join_rows(part):
    return part.reshape(part.shape[-2], part.shape[-1])


def scatter_weight(keep, send, order):
    got = swap(send, "seq", 1)
    part = (keep.astype(F32) + got.astype(F32)).astype(BF16)
    half = part.shape[1] // 2
    return scatter_chip(part[:, :half], part[:, half:], order)


def scatter_chip(mine, other, order):
    mine, other = split_rows(mine), split_rows(other)
    for at, name in enumerate(order):
        if name == "x":
            got = swap(other, "seq", 2)
            mine = (mine.astype(F32) + got.astype(F32)).astype(BF16)
            other = None
        elif other is None:
            mine = row_steps(mine, [name])
        else:
            both = row_steps(jnp.concatenate([mine, other], axis=-1), [name])
            half = both.shape[-1] // 2
            mine, other = both[..., :half], both[..., half:]
    return join_rows(mine).astype(F32)


def column_blocks(matrix, seq_here):
    width = matrix.shape[1] // 4

    def block(index):
        return lax.dynamic_slice_in_dim(matrix, index * width, width, 1)

    keep = jnp.concatenate([block(seq_here), block(seq_here ^ 2)], axis=1)
    send = jnp.concatenate([block(seq_here ^ 1), block(seq_here ^ 3)], axis=1)
    return keep, send


def weight_grad(rows_left, rows_right, seq_here, order):
    keep, send = column_blocks(rows_right, seq_here)
    return scatter_weight(
        dot_tn(rows_left, keep).astype(BF16), dot_tn(rows_left, send).astype(BF16), order
    )


def body(
    tokens_in,
    lengths,
    ln1_gain,
    ln1_bias,
    w_qkv,
    bias_query,
    bias_value,
    w_out,
    bias_out,
    ln2_gain,
    ln2_bias,
    w_up,
    bias_up,
    w_down,
    bias_down,
    proj_patch,
    proj_class,
    class_emb,
    d_masks,
):
    row_count, model_width = tokens_in.shape
    head_count = model_width // HEAD_DIM
    heads_here = head_count // 2
    third = model_width // 4
    seq_devices = lax.axis_size("seq")
    grp_devices = lax.axis_size("grp")
    mask_scale = math.sqrt(model_width)
    seq_here = lax.axis_index("seq")
    grp_here = lax.axis_index("grp")
    core = seq_here & 1
    length_here = lengths[0]
    bits = grp_devices.bit_length() - 1
    order_a = ["x"] + list(range(bits))
    order_b = [0, "x"] + list(range(1, bits))
    order_c = list(range(1, bits)) + ["x", 0]

    tokens_x = swap(tokens_in, "seq", 2)
    tokens_c = swap(tokens_in, "seq", 1)
    tokens_xc = swap(tokens_x, "seq", 1)
    image_rows = jnp.concatenate([tokens_in, tokens_c, tokens_x, tokens_xc], axis=0)
    within = jnp.arange(row_count, dtype=jnp.int32)
    positions = jnp.concatenate(
        [(seq_here ^ block) * row_count + within for block in range(seq_devices)]
    )
    key_keep = positions < length_here
    valid_rows = key_keep[:row_count].astype(F32)

    tokens = tokens_in.astype(F32)
    normed_image = layer_norm(image_rows.astype(F32), ln1_gain, ln1_bias).astype(BF16)
    norm_one_back = jax.vjp(layer_norm, tokens, ln1_gain, ln1_bias)[1]

    def own_heads(matrix):
        parts = matrix.reshape(matrix.shape[:-1] + (2, 2, third))
        parts = lax.dynamic_index_in_dim(parts, core, parts.ndim - 2, keepdims=False)
        return parts.reshape(matrix.shape[:-1] + (heads_here, HEAD_DIM))

    def low_half(matrix):
        return jnp.concatenate([matrix, jnp.zeros_like(matrix)], axis=-1)

    def high_half(matrix):
        return jnp.concatenate([jnp.zeros_like(matrix), matrix], axis=-1)

    def flat(matrix):
        return matrix.reshape(matrix.shape[:-2] + (heads_here * LANES,))

    wq = own_heads(w_qkv[:, :model_width])
    wk = own_heads(w_qkv[:, model_width : 2 * model_width])
    wv = own_heads(w_qkv[:, 2 * model_width :])
    column = jnp.arange(heads_here * LANES, dtype=jnp.int32) % LANES
    query_rows = (
        dot_nn(normed_image[: 2 * row_count], flat(high_half(wq)))
        + flat(high_half(own_heads(bias_query)))
    ).astype(BF16)
    query_rows = jnp.where(column == 0, 1.0, query_rows * HEAD_DIM**-0.5).astype(BF16)
    key_rows = dot_nn(normed_image, flat(high_half(wk))).astype(BF16)
    key_rows = jnp.where(
        column == 0, jnp.where(key_keep, 0.0, NEG_FILL)[:, None], key_rows
    ).astype(BF16)
    value_rows = (
        dot_nn(normed_image, flat(low_half(wv)))
        + flat(low_half(own_heads(bias_value)))
        + (column == HEAD_DIM).astype(F32)
    ).astype(BF16)

    att_t, mass = attend_forward(query_rows, key_rows, value_rows)
    att_got = swap(att_t[:, row_count:], "seq", 1)
    att_own = att_t[:, :row_count].reshape(2, third, row_count)
    att_got = att_got.reshape(2, third, row_count)
    first = jnp.where(core == 0, att_own, att_got)
    second = jnp.where(core == 0, att_got, att_own)
    attended_t = jnp.stack([first, second], axis=1).reshape(model_width, row_count)

    branch = dot_tn(attended_t, w_out) + bias_out
    middle = tokens + branch
    normed_two, norm_two_back = jax.vjp(layer_norm, middle, ln2_gain, ln2_bias)
    normed_two_low = normed_two.astype(BF16)
    hidden = dot_nn(normed_two_low, w_up) + bias_up
    active, gelu_back = jax.vjp(gelu_exact, hidden)
    active_low = active.astype(BF16)
    final = middle + (dot_nn(active_low, w_down) + bias_down)
    final_low = final.astype(BF16)
    patches = dot_nn(final_low, proj_patch)
    patch_unit, patch_back = jax.vjp(unit_rows, patches)
    patch_low = patch_unit.astype(BF16)
    classes = dot_nn(class_emb, proj_class)
    class_unit, class_back = jax.vjp(unit_rows, classes)
    class_low = class_unit.astype(BF16)
    mask_out = (dot_nt(patch_low, class_low) * mask_scale * valid_rows[:, None]).astype(BF16)
    mask_grad = (d_masks.astype(F32) * valid_rows[:, None]).astype(BF16)
    grad_patch_unit = dot_nn(mask_grad, class_low) * mask_scale
    class_part = dot_tn(mask_grad, patch_low) * mask_scale
    class_total = lax.psum(class_part, ("grp", "seq"))
    grad_classes = class_back(class_total)[0].astype(BF16)
    grad_patches = patch_back(grad_patch_unit)[0].astype(BF16)
    grad_final = dot_nt(grad_patches, proj_patch)
    grad_feed = grad_final.astype(BF16)
    grad_bias_down = column_sum(grad_feed)
    out_w_down = weight_grad(active_low, grad_feed, seq_here, order_a)
    out_proj_patch = weight_grad(final_low, grad_patches, seq_here, order_c)
    grad_active = dot_nt(grad_feed, w_down)
    grad_hidden = gelu_back(grad_active)[0].astype(BF16)
    out_w_up = weight_grad(normed_two_low, grad_hidden, seq_here, order_b)
    grad_bias_up = column_sum(grad_hidden)
    grad_normed_two = dot_nt(grad_hidden, w_up)
    grad_middle_norm, grad_ln2_gain, grad_ln2_bias = norm_two_back(grad_normed_two)
    grad_middle = grad_final + grad_middle_norm
    grad_branch = grad_middle.astype(BF16)
    out_w_out = weight_grad(attended_t.T, grad_branch, seq_here, order_c)
    grad_bias_out = column_sum(grad_branch)

    branch_got = swap(grad_branch, "seq", 1)
    branch_rows = jnp.concatenate([grad_branch, branch_got], axis=0)
    wo = own_heads(w_out.T)
    gout_rows = dot_nn(branch_rows, flat(low_half(wo))).astype(BF16)
    gq_t, gkv = attend_backward(query_rows, gout_rows, att_t, mass, key_rows, value_rows)

    w_pairs = flat(jnp.concatenate([wv, wk], axis=-1))
    w_query = wq.reshape(model_width, heads_here * HEAD_DIM)
    gq = gq_t.T
    gn_far = dot_nt(gkv[2 * row_count :], w_pairs)
    gn_near = dot_nt(gkv[: 2 * row_count], w_pairs) + dot_nt(gq, w_query)
    far_got = swap(gn_far[row_count:].astype(BF16), "seq", 1)
    far_sum = (gn_far[:row_count] + far_got.astype(F32)).astype(BF16)
    near_got = swap(gn_near[row_count:].astype(BF16), "seq", 1)
    x_got = swap(far_sum, "seq", 2)
    grad_normed_one = gn_near[:row_count] + near_got.astype(F32) + x_got.astype(F32)
    grad_tokens_norm, grad_ln1_gain, grad_ln1_bias = norm_one_back(grad_normed_one)
    grad_tokens = (grad_middle + grad_tokens_norm).astype(BF16)

    dw_q = dot_tn(normed_image[: 2 * row_count], gq)
    dw_kv = dot_tn(normed_image, gkv).reshape(model_width, heads_here, 2, HEAD_DIM)
    dw_v = dw_kv[:, :, 0].reshape(model_width, heads_here * HEAD_DIM)
    dw_k = dw_kv[:, :, 1].reshape(model_width, heads_here * HEAD_DIM)
    part_zero = jnp.concatenate([dw_q, dw_k[:, :third]], axis=1).astype(BF16)
    part_one = jnp.concatenate([dw_k[:, third:], dw_v], axis=1).astype(BF16)
    at_zero = seq_here < 2
    qkv_mine = jnp.where(at_zero, part_zero, part_one)
    qkv_other = jnp.where(at_zero, part_one, part_zero)
    qkv_rows = scatter_chip(qkv_mine, qkv_other, order_a)
    pieces = [qkv_rows[:, i * third : (i + 1) * third] for i in range(3)]
    piece_got = swap(jnp.where(core == 0, pieces[2], pieces[0]), "seq", 1)
    out_w_qkv = jnp.concatenate(
        [
            jnp.where(core == 0, pieces[0], pieces[1]),
            piece_got,
            jnp.where(core == 0, pieces[1], pieces[2]),
        ],
        axis=1,
    )

    def place(vector):
        halves = vector.reshape(2, 1, third)
        zero = jnp.zeros_like(halves)
        both = jnp.where(
            core == 0,
            jnp.concatenate([halves, zero], axis=1),
            jnp.concatenate([zero, halves], axis=1),
        )
        return both.reshape(model_width)

    grad_bias_query = place(column_sum(gq))
    gkv_sums = column_sum(gkv).reshape(heads_here, 2, HEAD_DIM)
    grad_bias_value = place(gkv_sums[:, 0].reshape(heads_here * HEAD_DIM))

    early = lax.psum(
        jnp.concatenate(
            [grad_bias_down, grad_bias_out, grad_ln2_gain, grad_ln2_bias, grad_bias_up]
        ),
        ("grp", "seq"),
    )
    late = lax.psum(
        jnp.concatenate([grad_ln1_gain, grad_ln1_bias, grad_bias_query, grad_bias_value]),
        ("grp", "seq"),
    )
    rows_each = model_width // grp_devices
    cols_each = model_width // seq_devices

    def vector_rows(packed, index):
        return lax.dynamic_slice_in_dim(
            packed, index * model_width + grp_here * rows_each, rows_each, 0
        )

    ff_each = bias_up.shape[0] // grp_devices
    out_bias_up = lax.dynamic_slice_in_dim(
        early, 4 * model_width + grp_here * ff_each, ff_each, 0
    )
    emb_cols = lax.dynamic_slice_in_dim(class_emb, grp_here * rows_each, rows_each, 1)
    class_cols = lax.dynamic_slice_in_dim(grad_classes, seq_here * cols_each, cols_each, 1)
    grad_proj_class = dot_tn(emb_cols, class_cols)
    proj_rows = lax.dynamic_slice_in_dim(proj_class, grp_here * rows_each, rows_each, 0)
    grad_class_emb = dot_nt(grad_classes, proj_rows)
    return (
        mask_out,
        grad_tokens,
        vector_rows(late, 0),
        vector_rows(late, 1),
        out_w_qkv,
        vector_rows(late, 2),
        vector_rows(late, 3),
        out_w_out,
        vector_rows(early, 1),
        vector_rows(early, 2),
        vector_rows(early, 3),
        out_w_up,
        out_bias_up,
        out_w_down,
        vector_rows(early, 0),
        out_proj_patch,
        grad_proj_class,
        grad_class_emb,
    )


def solution(mesh):
    rows = P(("grp", "seq"), None)
    both = P("grp", "seq")
    return jax.shard_map(
        body,
        mesh=mesh,
        in_specs=(rows, P("grp")) + (P(),) * 16 + (rows,),
        out_specs=(
            rows,
            rows,
            P("grp"),
            P("grp"),
            both,
            P("grp"),
            P("grp"),
            both,
            P("grp"),
            P("grp"),
            P("grp"),
            both,
            P("grp"),
            both,
            P("grp"),
            both,
            both,
            P(None, "grp"),
        ),
        check_vma=False,
    )
```

time: 1570 us -> 668 us (0.43)
  waiting for transfers between devices: 671 us -> 183 us
  matrix products: 526 us -> 130 us
  Pallas kernels: 0 us -> 142 us
  local copies, waits for them, and re-layouts: 171 us -> 52.9 us
  other arithmetic: 131 us -> 56.1 us
  starting transfers between devices: 1.3 us -> 37.1 us
    reduce_scatter x8 -> x0, waiting for transfers between devices: 495 us -> none  [the longest x1 166 us: body(): lax.psum_scatter(grad_w_down, 'grp', scatter_dimension=0, tiled=True)]
    dot_general x63 -> x30, matrix products: 526 us -> 130 us  [the longest x9 53 us: dot_nn(): lax.dot_general(a, b, (((1,), (0,)), ((), ())), preferred_element_type=F32)]
    pallas_call x0 -> x2, Pallas kernels: none -> 142 us  [the longest x1 99.2 us: attend_backward(): pl.pallas_call(attend_backward_kernel, grid=(heads, span // tile), in_spe...]
    ppermute x0 -> x33, waiting for transfers between devices: none -> 70.7 us  [swap(): return lax.ppermute(value, axis, [(i, i ^ bit) for i in range(size)])]
    unnamed x148 -> x201, local copies, waits for them, and re-layouts: 81.5 us -> 12.8 us
    reduce_sum x8 -> x3, other arithmetic: 67.2 us -> 3.55 us  [column_sum(): return jnp.sum(matrix_low.astype(F32), axis=0)]
    ppermute x0 -> x33, starting transfers between devices: none -> 37 us  [swap(): return lax.ppermute(value, axis, [(i, i ^ bit) for i in range(size)])]
    unnamed x1 -> x0, blocking collectives: 36.8 us -> none
  transfers between devices with their start and end apart: 15 -> 34, of which waited for: 9 -> 15; matrix products, arithmetic and copies ran while one was open for 41% -> 21% of each run, Pallas kernels for 0% -> 15%
where the time goes in v1:
time: 668 us; the launch traced here: 658 us
  waiting for transfers between devices  183 us (27%)
  Pallas kernels  142 us (21%)
  matrix products  130 us (19%)
  other arithmetic  56.1 us (8%)
  local copies, waits for them, and re-layouts  52.9 us (8%)
  blocking collectives  41 us (6%)
  starting transfers between devices  37.1 us (6%)
  between operations  16.7 us (2%)
    psum x1, waiting for transfers between devices, body(): class_total = lax.psum(class_part, ('grp', 'seq'))  112 us
    pallas_call x1, Pallas kernels, attend_backward(): pl.pallas_call(attend_backward_kernel, grid=(heads, span // tile), in_spe...  99.2 us
    ppermute x33, waiting for transfers between devices, swap(): return lax.ppermute(value, axis, [(i, i ^ bit) for i in range(size)])  70.7 us
    dot_general x9, matrix products, dot_nn(): lax.dot_general(a, b, (((1,), (0,)), ((), ())), preferred_element_type=F32)  53 us
    pallas_call x1, Pallas kernels, attend_forward(): pl.pallas_call(attend_forward_kernel, grid=(heads, 2), in_specs=[pl.Block...  42.6 us
    psum x1, blocking collectives, body(): lax.psum(jnp.concatenate([grad_ln1_gain, grad_ln1_bias, grad_bias_query,...  41 us
    dot_general x13, matrix products, dot_tn(): lax.dot_general(a, b, (((0,), (0,)), ((), ())), preferred_element_type=F32)  39.9 us
    dot_general x8, matrix products, dot_nt(): lax.dot_general(a, b, (((1,), (1,)), ((), ())), preferred_element_type=F32)  37.4 us
  transfers between devices with their start and end apart: 34, of which 15 were waited for; matrix products, arithmetic and copies ran while one was open for 21% of the time, Pallas kernels for 15%

profile of v1, /device:TPU:0, one launch (start us, length us, event | category | flops | bytes accessed | tf_op | source)
XLA Modules:
  0.0 658.5 jit_solution(16656006344318307748)
XLA Ops:
  7.8 2.6 collective-permute-start.1
  12.7 3.2 fusion.120
  15.9 2.4 copy.205
  23.1 2.4 constant_dynamic-slice_fusion.28
  26.6 10.6 %collective-permute-done.1 = bf16[768,768]{1,0:T(8,128)(2,1)} collective-permute-done((bf16[768,768]{1,0:T(8,128)(2,1)}, bf16[768,768]{1,0:T(8,128)(2,1)}, u32[]{:S(2)}, u32[]{:S(2)}) %collective-permute-start.1) | collective-permute-done | bytes 1179680 | tf_op jit(solution)/shard_map/ppermute | solution.py:191
  38.5 1.6 concatenate.111
  40.1 3.0 pad_maximum_fusion.2
  45.5 3.5 convert_reduce_fusion
  49.0 6.6 %fusion.2 = f32[3072]{0:T(1024)S(1)} fusion(f32[3072]{0:T(1024)S(1)} %broadcast_multiply_fusion, bf16[768,768]{1,0:T(8,128)(2,1)} %collective-permute-done.2, bf16[768,768]{1,0:T(8,128)(2,1)} %collective-permute-done.1, bf16[768,768]{1,0:T(8,128)(2,1)} %collective-permute-done, bf16[768,768]{1,0:T(8,128)(2,1)S(1)} %copy-done.9), kind=kLoop, calls=%fused_computation.5 | loop fusion | flops 25949184 | bytes 4743168 | tf_op jit(solution)/shard_map/reduce_sum | solution.py:171
  55.7 6.0 fusion.5
  61.8 2.0 fusion.17.q_ref
  63.8 5.8 broadcast_select_fusion.k_ref
  69.7 5.6 add_convert_fusion.1.v_ref
  75.3 42.6 %attend_forward.1 = (bf16[384,1536]{1,0:T(8,128)(2,1)S(1)}, f32[6,1,1536]{2,1,0:T(1,128)S(1)}) custom-call(bf16[1536,768]{1,0:T(8,128)(2,1)S(1)} %fusion.17.q_ref, bf16[3072,768]{1,0:T(8,128)(2,1)} %broadcast_select_fusion.k_ref, bf16[3072,768]{1,0:T(8,128)(2,1)} %add_convert_fusion.1.v_ref), custom_call_target="tpu_custom_call" | custom-call | flops 28991029248 | bytes 11796480 | tf_op jit(solution)/shard_map/attend_forward/pallas_call | solution.py:49
  120.3 2.2 concatenate.118
  123.1 1.7 fusion.79
  128.9 25.7 %multiply_convert_fusion = (bf16[768,3072]{1,0:T(8,128)(2,1)S(1)}, f32[768,3072]{1,0:T(8,128)}, f32[768,3072]{1,0:T(8,128)}) fusion(f32[3072]{0:T(1024)S(1)} %copy-done.73, bf16[768,768]{0,1:T(8,128)(2,1)S(1)} %add_convert_fusion.8, bf16[768,3072]{1,0:T(8,128)(2,1)S(1)} %bitcast.164), kind=kOutput, calls=%fused_computation.13 | convolution fusion | flops 3779592192 | bytes 29503488 | tf_op jit(solution)/shard_map/dot_general | solution.py:23
  154.6 2.1 copy-done.78
  156.8 4.1 add_convert_fusion.7
  165.9 12.8 %convert_reduce_fusion.1 = (f32[3072]{0:T(1024)}, bf16[768,3072]{1,0:T(8,128)(2,1)S(1)}) fusion(f32[768,3072]{1,0:T(8,128)} %get-tuple-element.156, f32[768,3072]{1,0:T(8,128)} %get-tuple-element.213, f32[3072]{0:T(1024)S(1)} %copy-done.73, bf16[768,768]{0,1:T(8,128)(2,1)S(1)} %get-tuple-element.151, bf16[3072,768]{1,0:T(8,128)(2,1)} %param.32), kind=kOutput, calls=%fused_computation.10 | convolution fusion | flops 3663983616 | bytes 29515776 | tf_op jit(solution)/shard_map/dot_general | solution.py:27
  178.7 9.1 %multiply_reduce_fusion = (f32[768]{0:T(1024)}, f32[768]{0:T(1024)S(1)}, f32[768]{0:T(1024)S(1)}, f32[768,768]{0,1:T(8,128)S(1)}) fusion(f32[768,768]{0,1:T(8,128)S(1)} %get-tuple-element.212, f32[768]{0:T(1024)S(1)} %fusion.103, f32[768]{0:T(1024)S(1)} %broadcast_multiply_fusion.3, f32[768]{0:T(1024)S(1)} %copy-done.59, ...), kind=kOutput, calls=%fused_computation.79 | convolution fusion | flops 3628594944 | bytes 14174208 | tf_op jit(solution)/shard_map/dot_general | solution.py:27
  190.3 2.3 constant_dynamic-slice_fusion.24
  194.0 2.7 convolution_convert_fusion.6
  197.3 6.1 convolution_convert_fusion.1
  205.4 1.9 constant_dynamic-slice_fusion.18
  207.3 3.4 convolution_convert_fusion.3
  212.0 111.9 %all-reduce.13.cloned.1.call-done = f32[150,768]{1,0:T(8,128)} async-done(((f32[150,768]{1,0:T(8,128)}), f32[150,768]{1,0:T(8,128)}) %all-reduce.13.cloned.1.call-update) | async-done | bytes 460816 | tf_op jit(solution)/shard_map/psum | solution.py:371
  326.2 1.8 fusion.88
  328.0 1.8 fusion.84
  329.8 1.7 add_convert_fusion.10
  332.1 2.8 collective-permute-start.29
  334.9 1.7 add_convert_fusion.13
  338.0 4.8 collective-permute-done.29
  343.0 2.6 collective-permute-start.30
  345.6 5.3 collective-permute-done.14
  352.8 4.9 collective-permute-done.15
  360.1 2.4 collective-permute-done.16
  364.8 2.0 collective-permute-done.17
  367.4 5.4 convolution_convert_fusion.5.gout_ref
  372.9 99.2 %attend_backward.1 = (bf16[384,1536]{1,0:T(8,128)(2,1)}, bf16[3072,768]{1,0:T(8,128)(2,1)}) custom-call(bf16[1536,768]{1,0:T(8,128)(2,1)} %copy-done.3, bf16[1536,768]{1,0:T(8,128)(2,1)} %convolution_convert_fusion.5.gout_ref, bf16[384,1536]{1,0:T(8,128)(2,1)} %copy-done.2, f32[6,1,1536]{2,1,0:T(1,128)} %copy-done.4, ...), custom_call_target="tpu_custom_call" | custom-call | flops 72477573120 | bytes 18874368 | tf_op jit(solution)/shard_map/attend_backward/pallas_call | solution.py:132
  473.6 2.7 fusion.42
  476.3 7.8 %fusion.130 = bf16[768,768]{0,1:T(8,128)(2,1)S(1)} fusion(bf16[3072,768]{1,0:T(8,128)(2,1)} %copy-done.18, bf16[3072,768]{1,0:T(8,128)(2,1)} %get-tuple-element.24), kind=kOutput, calls=%fused_computation.301 | convolution fusion | flops 3623878656 | bytes 10616832 | tf_op jit(solution)/shard_map/dot_general | solution.py:31
  489.4 4.0 fusion.37
  493.4 3.7 convolution_add_fusion
  498.1 3.0 slice.214
  501.1 3.9 fusion.35
  506.9 2.5 add_convert_fusion.9
  510.9 3.7 add_convert_fusion.2
  514.6 1.8 fusion.121
  520.1 4.2 add_convert_fusion.3
  526.1 2.6 collective-permute-start.10
  529.1 3.7 collective-permute-done.10
  532.9 4.5 collective-permute-start.11
  537.4 2.7 fusion.23
  541.9 4.3 reshape.388
  547.9 2.8 fusion.34
  556.6 16.6 %collective-permute-done.7 = bf16[768,768]{0,1:T(8,128)(2,1)} collective-permute-done((bf16[768,768]{0,1:T(8,128)(2,1)}, bf16[768,768]{0,1:T(8,128)(2,1)}, u32[]{:S(2)}, u32[]{:S(2)}) %collective-permute-start.7) | collective-permute-done | bytes 1179680 | tf_op jit(solution)/shard_map/ppermute | solution.py:191
  573.2 2.7 fusion.18
  580.0 41.0 %all-reduce.10 = (f32[3072]{0:T(1024)S(1)}, f32[6144]{0:T(1024)S(1)}) all-reduce(f32[3072]{0:T(1024)S(1)} %pad_maximum_fusion.6, f32[6144]{0:T(1024)S(1)} %copy-done.58), channel_id=1, replica_groups=mesh['grp'=8,'seq'=4] {'grp','seq'}, use_global_device_ids=true, to_apply=%region_17.18 | all-reduce | flops 9216 | bytes 73728 | tf_op jit(solution)/shard_map/psum | solution.py:450
  624.4 2.1 collective-permute-start.26
  626.8 7.6 %collective-permute-done.26 = bf16[2,1,1,384,192]{3,4,2,1,0:T(8,128)(2,1)S(1)} collective-permute-done((bf16[2,1,1,384,192]{3,4,2,1,0:T(8,128)(2,1)S(1)}, bf16[2,1,1,384,192]{3,4,2,1,0:T(8,128)(2,1)S(1)}, u32[]{:S(2)}, u32[]{:S(2)}) %collective-permute-start.26) | collective-permute-done | bytes 294944 | tf_op jit(solution)/shard_map/ppermute | solution.py:191
  634.5 2.9 collective-permute-start.27
  637.4 4.8 collective-permute-done.21
  644.3 6.2 collective-permute-done.22
  (378 shorter events, 79.7 us)
Async XLA Ops:
  7.2 153.7 %copy-start = (bf16[768,768]{1,0:T(8,128)(2,1)S(1)}, bf16[768,768]{1,0:T(8,128)(2,1)}, u32[]{:S(2)}) copy-start(bf16[768,768]{1,0:T(8,128)(2,1)} %param.34) | copy-start | bytes 3538948
  7.2 316.7 %all-reduce.13.cloned.1.call-start = ((), (), s32[]{:S(2)}) async-start(), calls=%async_computation | async-start | bytes 933888 | tf_op jit(solution)/shard_map/psum | solution.py:371
  7.3 38.2 %collective-permute-start = (bf16[768,768]{1,0:T(8,128)(2,1)}, bf16[768,768]{1,0:T(8,128)(2,1)}, u32[]{:S(2)}, u32[]{:S(2)}) collective-permute-start(bf16[768,768]{1,0:T(8,128)(2,1)} %param.19), channel_id=1, source_target_pairs={{0,1},{1,0},{2,3},{3,2},{4,5},{5,4},{6,7},{7,6},{8,9},{9,8},{10,11... | collective-permute-start | bytes 3538952 | tf_op jit(solution)/shard_map/ppermute | solution.py:191
  7.8 29.4 %collective-permute-start.1 = (bf16[768,768]{1,0:T(8,128)(2,1)}, bf16[768,768]{1,0:T(8,128)(2,1)}, u32[]{:S(2)}, u32[]{:S(2)}) collective-permute-start(bf16[768,768]{1,0:T(8,128)(2,1)} %param.19), channel_id=1, source_target_pairs={{0,2},{1,3},{2,0},{3,1},{4,6},{5,7},{6,4},{7,5},{8,10},{9,11},{10,... | collective-permute-start | bytes 3538952 | tf_op jit(solution)/shard_map/ppermute | solution.py:191
  23.1 14.7 %copy-start.9 = (bf16[768,768]{1,0:T(8,128)(2,1)S(1)}, bf16[768,768]{1,0:T(8,128)(2,1)}, u32[]{:S(2)}) copy-start(bf16[768,768]{1,0:T(8,128)(2,1)} %param.19) | copy-start | bytes 3538948
  37.2 8.3 %collective-permute-start.2 = (bf16[768,768]{1,0:T(8,128)(2,1)}, bf16[768,768]{1,0:T(8,128)(2,1)}, u32[]{:S(2)}, u32[]{:S(2)}) collective-permute-start(bf16[768,768]{1,0:T(8,128)(2,1)} %collective-permute-done.1), channel_id=1, source_target_pairs={{0,1},{1,0},{2,3},{3,2},{4,5},{5,4},{6,7},{7,6},{8,9},{9,8},{10,11... | collective-permute-start | bytes 3538952 | tf_op jit(solution)/shard_map/ppermute | solution.py:191
  38.5 87.8 %copy-start.5 = (bf16[768,768]{0,1:T(8,128)(2,1)}, bf16[768,768]{0,1:T(8,128)(2,1)S(1)}, u32[]{:S(2)}) copy-start(bf16[768,768]{0,1:T(8,128)(2,1)S(1)} %copy.164) | copy-start | bytes 3538948
  44.9 78.2 %copy-start.60 = (f32[150]{0:T(256)}, f32[150]{0:T(256)S(1)}, u32[]{:S(2)}) copy-start(f32[150]{0:T(256)S(1)} %add_rsqrt_fusion.2) | copy-start | bytes 1804
  44.9 78.2 %copy-start.52 = (f32[768]{0:T(1024)}, f32[768]{0:T(1024)S(1)}, u32[]{:S(2)}) copy-start(f32[768]{0:T(1024)S(1)} %slice_convert_fusion.3) | copy-start | bytes 9220
  63.8 11.5 %copy-start.3 = (bf16[1536,768]{1,0:T(8,128)(2,1)}, bf16[1536,768]{1,0:T(8,128)(2,1)S(1)}, u32[]{:S(2)}) copy-start(bf16[1536,768]{1,0:T(8,128)(2,1)S(1)} %fusion.17.q_ref) | copy-start | bytes 7077892
  119.5 5.4 collective-permute-start.3
  127.7 29.1 %slice-start.10 = ((s8[4718592]{0:T(1024)(128)(4,1)}), s8[4194304]{0:T(1024)(128)(4,1)S(1)}, s32[]{:S(2)}) async-start(s8[4718592]{0:T(1024)(128)(4,1)} %bitcast.161), calls=%async_computation.11 | async-start | bytes 8388608
  128.8 25.8 %copy-start.30 = (bf16[768,768]{0,1:T(8,128)(2,1)}, bf16[768,768]{0,1:T(8,128)(2,1)S(1)}, u32[]{:S(2)}) copy-start(bf16[768,768]{0,1:T(8,128)(2,1)S(1)} %add_convert_fusion.8) | copy-start | bytes 3538948
  128.8 27.9 %slice-start.11 = ((s8[4718592]{0:T(1024)(128)(4,1)}), s8[524288]{0:T(1024)(128)(4,1)S(1)}, s32[]{:S(2)}) async-start(s8[4718592]{0:T(1024)(128)(4,1)} %bitcast.161), calls=%async_computation.12 | async-start | bytes 1048576
  128.9 27.9 %copy-start.75 = (f32[768]{0:T(1024)S(1)}, f32[768]{0:T(1024)}, u32[]{:S(2)}) copy-start(f32[768]{0:T(1024)} %param.33) | copy-start | bytes 9220
  163.8 24.6 %copy-start.13 = (f32[768,768]{0,1:T(8,128)}, f32[768,768]{0,1:T(8,128)S(1)}, u32[]{:S(2)}) copy-start(f32[768,768]{0,1:T(8,128)S(1)} %get-tuple-element.217) | copy-start | bytes 7077892
  192.6 174.8 %collective-permute-start.4 = (bf16[768,768]{0,1:T(8,128)(2,1)}, bf16[768,768]{0,1:T(8,128)(2,1)}, u32[]{:S(2)}, u32[]{:S(2)}) collective-permute-start(bf16[768,768]{0,1:T(8,128)(2,1)} %get-tuple-element.149), channel_id=1, source_target_pairs={{0,1},{1,0},{2,3},{3,2},{4,5},{5,4},{6,7},{7,6},{8,9},{9,8},{10,11... | collective-permute-start | bytes 3538952 | tf_op jit(solution)/shard_map/ppermute | solution.py:191
  196.7 133.1 %collective-permute-start.28 = (bf16[768,384]{0,1:T(8,128)(2,1)}, bf16[768,384]{0,1:T(8,128)(2,1)}, u32[]{:S(2)}, u32[]{:S(2)}) collective-permute-start(bf16[768,384]{0,1:T(8,128)(2,1)} %convolution_convert_fusion.6), channel_id=1, source_target_pairs={{0,1},{1,0},{2,3},{3,2},{4,5},{5,4},{6,7},{7,6},{8,9},{9,8},{10,11... | collective-permute-start | bytes 1769480 | tf_op jit(solution)/shard_map/ppermute | solution.py:191
  203.3 307.5 %collective-permute-start.23 = (bf16[3072,384]{0,1:T(8,128)(2,1)}, bf16[3072,384]{0,1:T(8,128)(2,1)}, u32[]{:S(2)}, u32[]{:S(2)}) collective-permute-start(bf16[3072,384]{0,1:T(8,128)(2,1)} %convolution_convert_fusion.1), channel_id=1, source_target_pairs={{0,1},{1,0},{2,3},{3,2},{4,5},{5,4},{6,7},{7,6},{8,9},{9,8},{10,11... | collective-permute-start | bytes 7077896 | tf_op jit(solution)/shard_map/ppermute | solution.py:191
  204.9 130.1 %collective-permute-start.13 = (bf16[768,384]{0,1:T(8,128)(2,1)}, bf16[768,384]{0,1:T(8,128)(2,1)}, u32[]{:S(2)}, u32[]{:S(2)}) collective-permute-start(bf16[768,384]{0,1:T(8,128)(2,1)} %convolution_convert_fusion.8), channel_id=1, source_target_pairs={{0,1},{1,0},{2,3},{3,2},{4,5},{5,4},{6,7},{7,6},{8,9},{9,8},{10,11... | collective-permute-start | bytes 1769480 | tf_op jit(solution)/shard_map/ppermute | solution.py:191
  210.7 114.3 %copy-start.65 = (f32[150]{0:T(256)S(1)}, f32[150]{0:T(256)}, u32[]{:S(2)}) copy-start(f32[150]{0:T(256)} %copy-done.64) | copy-start | bytes 1804
  210.7 309.4 %collective-permute-start.18 = (bf16[768,1536]{1,0:T(8,128)(2,1)}, bf16[768,1536]{1,0:T(8,128)(2,1)}, u32[]{:S(2)}, u32[]{:S(2)}) collective-permute-start(bf16[768,1536]{1,0:T(8,128)(2,1)} %convolution_convert_fusion.3), channel_id=1, source_target_pairs={{0,1},{1,0},{2,3},{3,2},{4,5},{5,4},{6,7},{7,6},{8,9},{9,8},{10,11... | collective-permute-start | bytes 7077896 | tf_op jit(solution)/shard_map/ppermute | solution.py:191
  210.9 114.1 %copy-start.57 = (f32[6144]{0:T(1024)}, f32[6144]{0:T(1024)S(1)}, u32[]{:S(2)}) copy-start(f32[6144]{0:T(1024)S(1)} %constant_dynamic-update-slice_fusion) | copy-start | bytes 73732
  210.9 118.9 %copy-start.43 = (bf16[768,192]{0,1:T(8,128)(2,1)S(1)}, bf16[768,192]{0,1:T(8,128)(2,1)}, u32[]{:S(2)}) copy-start(bf16[768,192]{0,1:T(8,128)(2,1)} %get-tuple-element.172) | copy-start | bytes 884740
  212.0 117.8 %copy-start.44 = (bf16[768,192]{0,1:T(8,128)(2,1)S(1)}, bf16[768,192]{0,1:T(8,128)(2,1)}, u32[]{:S(2)}) copy-start(bf16[768,192]{0,1:T(8,128)(2,1)} %get-tuple-element.175) | copy-start | bytes 884740
  212.0 117.8 %copy-start.77 = (bf16[768,768]{0,1:T(8,128)(2,1)S(1)}, bf16[768,768]{0,1:T(8,128)(2,1)}, u32[]{:S(2)}) copy-start(bf16[768,768]{0,1:T(8,128)(2,1)} %copy-done.76) | copy-start | bytes 3538948
  332.1 10.7 %collective-permute-start.29 = (bf16[2,1,2,96,384]{4,3,2,1,0:T(8,128)(2,1)S(1)}, bf16[2,1,2,96,384]{4,3,2,1,0:T(8,128)(2,1)S(1)}, u32[]{:S(2)}, u32[]{:S(2)}) collective-permute-start(bf16[2,1,2,96,384]{4,3,2,1,0:T(8,128)(2,1)S(1)} %fusion.75), channel_id=1, source_target_pairs={{0,8},{4,12},{8,0},{12,4},{16,24},{20,28},{24,16},{28,20},{1,9},{5... | collective-permute-start | bytes 884744 | tf_op jit(solution)/shard_map/ppermute | solution.py:191
  337.2 13.7 %collective-permute-start.14 = (bf16[2,1,2,96,384]{4,3,2,1,0:T(8,128)(2,1)S(1)}, bf16[2,1,2,96,384]{4,3,2,1,0:T(8,128)(2,1)S(1)}, u32[]{:S(2)}, u32[]{:S(2)}) collective-permute-start(bf16[2,1,2,96,384]{4,3,2,1,0:T(8,128)(2,1)S(1)} %fusion.77), channel_id=1, source_target_pairs={{0,8},{4,12},{8,0},{12,4},{16,24},{20,28},{24,16},{28,20},{1,9},{5... | collective-permute-start | bytes 884744 | tf_op jit(solution)/shard_map/ppermute | solution.py:191
  343.0 24.5 %copy-start.32 = (bf16[768,6,128]{0,2,1:T(8,128)(2,1)S(1)}, bf16[768,6,128]{0,2,1:T(8,128)(2,1)}, u32[]{:S(2)}) copy-start(bf16[768,6,128]{0,2,1:T(8,128)(2,1)} %concatenate.118) | copy-start | bytes 3538948
  343.0 8.1 %collective-permute-start.30 = (bf16[1,1,2,96,384]{4,3,2,1,0:T(8,128)(2,1)S(1)}, bf16[1,1,2,96,384]{4,3,2,1,0:T(8,128)(2,1)S(1)}, u32[]{:S(2)}, u32[]{:S(2)}) collective-permute-start(bf16[1,1,2,96,384]{4,3,2,1,0:T(8,128)(2,1)S(1)} %constant_dynamic-slice_fusion.1), channel_id=1, source_target_pairs={{0,16},{4,20},{8,24},{12,28},{16,0},{20,4},{24,8},{28,12},{1,17},{... | collective-permute-start | bytes 442376 | tf_op jit(solution)/shard_map/ppermute | solution.py:191
  351.1 6.7 %collective-permute-start.15 = (bf16[1,1,2,96,384]{4,3,2,1,0:T(8,128)(2,1)S(1)}, bf16[1,1,2,96,384]{4,3,2,1,0:T(8,128)(2,1)S(1)}, u32[]{:S(2)}, u32[]{:S(2)}) collective-permute-start(bf16[1,1,2,96,384]{4,3,2,1,0:T(8,128)(2,1)S(1)} %constant_dynamic-slice_fusion.20), channel_id=1, source_target_pairs={{0,16},{4,20},{8,24},{12,28},{16,0},{20,4},{24,8},{28,12},{1,17},{... | collective-permute-start | bytes 442376 | tf_op jit(solution)/shard_map/ppermute | solution.py:191
  351.3 8.1 %collective-permute-start.31 = (bf16[1,1,2,96,192]{4,3,2,1,0:T(8,128)(2,1)S(1)}, bf16[1,1,2,96,192]{4,3,2,1,0:T(8,128)(2,1)S(1)}, u32[]{:S(2)}, u32[]{:S(2)}) collective-permute-start(bf16[1,1,2,96,192]{4,3,2,1,0:T(8,128)(2,1)S(1)} %slice.179), channel_id=1, source_target_pairs={{0,2},{1,3},{2,0},{3,1},{4,6},{5,7},{6,4},{7,5},{8,10},{9,11},{10,... | collective-permute-start | bytes 221192 | tf_op jit(solution)/shard_map/ppermute | solution.py:191
  357.9 4.7 collective-permute-start.16
  359.5 4.7 collective-permute-start.32
  362.6 4.2 collective-permute-start.17
  367.4 106.1 %slice-start.4 = ((s8[4718592]{0:T(1024)(128)(4,1)}), s8[4194304]{0:T(1024)(128)(4,1)S(1)}, s32[]{:S(2)}) async-start(s8[4718592]{0:T(1024)(128)(4,1)} %bitcast.121), calls=%async_computation.5 | async-start | bytes 8388608
  372.9 100.7 %slice-start.5 = ((s8[4718592]{0:T(1024)(128)(4,1)}), s8[524288]{0:T(1024)(128)(4,1)S(1)}, s32[]{:S(2)}) async-start(s8[4718592]{0:T(1024)(128)(4,1)} %bitcast.121), calls=%async_computation.6 | async-start | bytes 1048576
  476.3 10.2 %copy-start.25 = (bf16[768,384]{1,0:T(8,128)(2,1)}, bf16[768,384]{1,0:T(8,128)(2,1)S(1)}, u32[]{:S(2)}) copy-start(bf16[768,384]{1,0:T(8,128)(2,1)S(1)} %fusion.42) | copy-start | bytes 1769476
  487.9 18.8 %collective-permute-start.8 = (bf16[2,2,2,96,576]{4,3,2,1,0:T(8,128)(2,1)}, bf16[2,2,2,96,576]{4,3,2,1,0:T(8,128)(2,1)}, u32[]{:S(2)}, u32[]{:S(2)}) collective-permute-start(bf16[2,2,2,96,576]{4,3,2,1,0:T(8,128)(2,1)} %broadcast_select_fusion.1), channel_id=1, source_target_pairs={{0,2},{1,3},{2,0},{3,1},{4,6},{5,7},{6,4},{7,5},{8,10},{9,11},{10,... | collective-permute-start | bytes 2654216 | tf_op jit(solution)/shard_map/ppermute | solution.py:191
  498.1 12.7 %slice-start.14 = ((s8[4718592]{0:T(1024)(128)(4,1)}), s8[4194304]{0:T(1024)(128)(4,1)S(1)}, s32[]{:S(2)}) async-start(s8[4718592]{0:T(1024)(128)(4,1)} %bitcast.165), calls=%async_computation.15 | async-start | bytes 8388608
  501.1 9.7 %slice-start.15 = ((s8[4718592]{0:T(1024)(128)(4,1)}), s8[524288]{0:T(1024)(128)(4,1)S(1)}, s32[]{:S(2)}) async-start(s8[4718592]{0:T(1024)(128)(4,1)} %bitcast.165), calls=%async_computation.16 | async-start | bytes 1048576
  506.2 31.2 %collective-permute-start.6 = (bf16[768,768]{0,1:T(8,128)(2,1)}, bf16[768,768]{0,1:T(8,128)(2,1)}, u32[]{:S(2)}, u32[]{:S(2)}) collective-permute-start(bf16[768,768]{0,1:T(8,128)(2,1)} %slice.213), channel_id=1, source_target_pairs={{0,1},{1,0},{2,3},{3,2},{4,5},{5,4},{6,7},{7,6},{8,9},{9,8},{10,11... | collective-permute-start | bytes 3538952 | tf_op jit(solution)/shard_map/ppermute | solution.py:191
  506.2 50.4 %collective-permute-start.5 = (bf16[768,768]{0,1:T(8,128)(2,1)}, bf16[768,768]{0,1:T(8,128)(2,1)}, u32[]{:S(2)}, u32[]{:S(2)}) collective-permute-start(bf16[768,768]{0,1:T(8,128)(2,1)} %slice.214), channel_id=1, source_target_pairs={{0,1},{1,0},{2,3},{3,2},{4,5},{5,4},{6,7},{7,6},{8,9},{9,8},{10,11... | collective-permute-start | bytes 3538952 | tf_op jit(solution)/shard_map/ppermute | solution.py:191
  510.2 14.2 %collective-permute-start.9 = (bf16[2,2,1,96,576]{4,3,2,1,0:T(8,128)(2,1)}, bf16[2,2,1,96,576]{4,3,2,1,0:T(8,128)(2,1)}, u32[]{:S(2)}, u32[]{:S(2)}) collective-permute-start(bf16[2,2,1,96,576]{4,3,2,1,0:T(8,128)(2,1)} %constant_dynamic-slice_fusion.27), channel_id=1, source_target_pairs={{0,4},{4,0},{8,12},{12,8},{16,20},{20,16},{24,28},{28,24},{1,5},{5... | collective-permute-start | bytes 1327112 | tf_op jit(solution)/shard_map/ppermute | solution.py:191
  518.7 29.2 %collective-permute-start.24 = (bf16[2,2,2,384,192]{3,4,2,1,0:T(8,128)(2,1)}, bf16[2,2,2,384,192]{3,4,2,1,0:T(8,128)(2,1)}, u32[]{:S(2)}, u32[]{:S(2)}) collective-permute-start(bf16[2,2,2,384,192]{3,4,2,1,0:T(8,128)(2,1)} %copy.186), channel_id=1, source_target_pairs={{0,2},{1,3},{2,0},{3,1},{4,6},{5,7},{6,4},{7,5},{8,10},{9,11},{10,... | collective-permute-start | bytes 3538952 | tf_op jit(solution)/shard_map/ppermute | solution.py:191
  520.1 17.3 %slice-start.8 = ((s8[4718592]{0:T(1024)(128)(4,1)}), s8[4194304]{0:T(1024)(128)(4,1)S(1)}, s32[]{:S(2)}) async-start(s8[4718592]{0:T(1024)(128)(4,1)} %bitcast.140), calls=%async_computation.9 | async-start | bytes 8388608
  520.1 17.3 %slice-start.9 = ((s8[4718592]{0:T(1024)(128)(4,1)}), s8[524288]{0:T(1024)(128)(4,1)S(1)}, s32[]{:S(2)}) async-start(s8[4718592]{0:T(1024)(128)(4,1)} %bitcast.140), calls=%async_computation.10 | async-start | bytes 1048576
  526.1 6.8 %collective-permute-start.10 = (bf16[2,1,1,96,576]{4,3,2,1,0:T(8,128)(2,1)S(1)}, bf16[2,1,1,96,576]{4,3,2,1,0:T(8,128)(2,1)S(1)}, u32[]{:S(2)}, u32[]{:S(2)}) collective-permute-start(bf16[2,1,1,96,576]{4,3,2,1,0:T(8,128)(2,1)S(1)} %constant_dynamic-slice_fusion.26), channel_id=1, source_target_pairs={{0,8},{4,12},{8,0},{12,4},{16,24},{20,28},{24,16},{28,20},{1,9},{5... | collective-permute-start | bytes 663560 | tf_op jit(solution)/shard_map/ppermute | solution.py:191
  528.7 24.4 %collective-permute-start.19 = (bf16[2,2,1,96,1536]{4,3,2,1,0:T(8,128)(2,1)S(1)}, bf16[2,2,1,96,1536]{4,3,2,1,0:T(8,128)(2,1)}, u32[]{:S(2)}, u32[]{:S(2)}) collective-permute-start(bf16[2,2,1,96,1536]{4,3,2,1,0:T(8,128)(2,1)S(1)} %fusion.48), channel_id=1, source_target_pairs={{0,4},{4,0},{8,12},{12,8},{16,20},{20,16},{24,28},{28,24},{1,5},{5... | collective-permute-start | bytes 3538952 | tf_op jit(solution)/shard_map/ppermute | solution.py:191
  532.9 8.7 %collective-permute-start.11 = (bf16[1,1,1,96,576]{4,3,2,1,0:T(8,128)(2,1)S(1)}, bf16[1,1,1,96,576]{4,3,2,1,0:T(8,128)(2,1)S(1)}, u32[]{:S(2)}, u32[]{:S(2)}) collective-permute-start(bf16[1,1,1,96,576]{4,3,2,1,0:T(8,128)(2,1)S(1)} %constant_dynamic-slice_fusion.25), channel_id=1, source_target_pairs={{0,16},{4,20},{8,24},{12,28},{16,0},{20,4},{24,8},{28,12},{1,17},{... | collective-permute-start | bytes 331784 | tf_op jit(solution)/shard_map/ppermute | solution.py:191
  540.1 33.1 %collective-permute-start.7 = (bf16[768,768]{0,1:T(8,128)(2,1)}, bf16[768,768]{0,1:T(8,128)(2,1)}, u32[]{:S(2)}, u32[]{:S(2)}) collective-permute-start(bf16[768,768]{0,1:T(8,128)(2,1)} %fusion.23), channel_id=1, source_target_pairs={{0,2},{1,3},{2,0},{3,1},{4,6},{5,7},{6,4},{7,5},{8,10},{9,11},{10,... | collective-permute-start | bytes 3538952 | tf_op jit(solution)/shard_map/ppermute | solution.py:191
  541.7 4.5 collective-permute-start.12
  541.9 31.3 %slice-start = ((s8[4718592]{0:T(1024)(128)(4,1)}), s8[524288]{0:T(1024)(128)(4,1)S(1)}, s32[]{:S(2)}) async-start(s8[4718592]{0:T(1024)(128)(4,1)} %bitcast.111), calls=%async_computation.1 | async-start | bytes 1048576
  547.0 26.2 %slice-start.1 = ((s8[4718592]{0:T(1024)(128)(4,1)}), s8[4194304]{0:T(1024)(128)(4,1)S(1)}, s32[]{:S(2)}) async-start(s8[4718592]{0:T(1024)(128)(4,1)} %bitcast.111), calls=%async_computation.2 | async-start | bytes 8388608
  551.7 21.5 %copy-start.6 = (bf16[768,768]{0,1:T(8,128)(2,1)S(1)}, bf16[768,768]{0,1:T(8,128)(2,1)}, u32[]{:S(2)}) copy-start(bf16[768,768]{0,1:T(8,128)(2,1)} %copy-done.5) | copy-start | bytes 3538948
  551.7 21.5 %copy-start.50 = (f32[768]{0:T(1024)S(1)}, f32[768]{0:T(1024)}, u32[]{:S(2)}) copy-start(f32[768]{0:T(1024)} %param.21) | copy-start | bytes 9220
  551.7 21.5 %copy-start.51 = (f32[768]{0:T(1024)S(1)}, f32[768]{0:T(1024)}, u32[]{:S(2)}) copy-start(f32[768]{0:T(1024)} %broadcast_multiply_fusion.2) | copy-start | bytes 9220
  551.7 71.2 %collective-permute-start.25 = (bf16[2,2,1,384,192]{3,4,2,1,0:T(8,128)(2,1)}, bf16[2,2,1,384,192]{3,4,2,1,0:T(8,128)(2,1)}, u32[]{:S(2)}, u32[]{:S(2)}) collective-permute-start(bf16[2,2,1,384,192]{3,4,2,1,0:T(8,128)(2,1)} %constant_dynamic-slice_fusion.8), channel_id=1, source_target_pairs={{0,4},{4,0},{8,12},{12,8},{16,20},{20,16},{24,28},{28,24},{1,5},{5... | collective-permute-start | bytes 1769480 | tf_op jit(solution)/shard_map/ppermute | solution.py:191
  555.6 70.9 %collective-permute-start.20 = (bf16[2,2,1,96,768]{4,3,2,1,0:T(8,128)(2,1)}, bf16[2,2,1,96,768]{4,3,2,1,0:T(8,128)(2,1)S(1)}, u32[]{:S(2)}, u32[]{:S(2)}) collective-permute-start(bf16[2,2,1,96,768]{4,3,2,1,0:T(8,128)(2,1)} %slice.173), channel_id=1, source_target_pairs={{0,2},{1,3},{2,0},{3,1},{4,6},{5,7},{6,4},{7,5},{8,10},{9,11},{10,... | collective-permute-start | bytes 1769480 | tf_op jit(solution)/shard_map/ppermute | solution.py:191
  624.4 10.0 %collective-permute-start.26 = (bf16[2,1,1,384,192]{3,4,2,1,0:T(8,128)(2,1)S(1)}, bf16[2,1,1,384,192]{3,4,2,1,0:T(8,128)(2,1)S(1)}, u32[]{:S(2)}, u32[]{:S(2)}) collective-permute-start(bf16[2,1,1,384,192]{3,4,2,1,0:T(8,128)(2,1)S(1)} %constant_dynamic-slice_fusion.7), channel_id=1, source_target_pairs={{0,8},{4,12},{8,0},{12,4},{16,24},{20,28},{24,16},{28,20},{1,9},{5... | collective-permute-start | bytes 884744 | tf_op jit(solution)/shard_map/ppermute | solution.py:191
  626.5 24.7 %copy-start.1 = (bf16[768,768]{1,0:T(8,128)(2,1)S(1)}, bf16[768,768]{1,0:T(8,128)(2,1)}, u32[]{:S(2)}) copy-start(bf16[768,768]{1,0:T(8,128)(2,1)} %param.34) | copy-start | bytes 3538948
  626.7 15.5 %collective-permute-start.21 = (bf16[2,1,1,96,768]{4,3,2,1,0:T(8,128)(2,1)S(1)}, bf16[2,1,1,96,768]{4,3,2,1,0:T(8,128)(2,1)S(1)}, u32[]{:S(2)}, u32[]{:S(2)}) collective-permute-start(bf16[2,1,1,96,768]{4,3,2,1,0:T(8,128)(2,1)S(1)} %constant_dynamic-slice_fusion.14), channel_id=1, source_target_pairs={{0,8},{4,12},{8,0},{12,4},{16,24},{20,28},{24,16},{28,20},{1,9},{5... | collective-permute-start | bytes 884744 | tf_op jit(solution)/shard_map/ppermute | solution.py:191
  634.5 9.0 %collective-permute-start.27 = (bf16[1,1,1,384,192]{3,4,2,1,0:T(8,128)(2,1)S(1)}, bf16[1,1,1,384,192]{3,4,2,1,0:T(8,128)(2,1)S(1)}, u32[]{:S(2)}, u32[]{:S(2)}) collective-permute-start(bf16[1,1,1,384,192]{3,4,2,1,0:T(8,128)(2,1)S(1)} %constant_dynamic-slice_fusion.6), channel_id=1, source_target_pairs={{0,16},{4,20},{8,24},{12,28},{16,0},{20,4},{24,8},{28,12},{1,17},{... | collective-permute-start | bytes 442376 | tf_op jit(solution)/shard_map/ppermute | solution.py:191
  642.3 8.2 %collective-permute-start.22 = (bf16[1,1,1,96,768]{4,3,2,1,0:T(8,128)(2,1)S(1)}, bf16[1,1,1,96,768]{4,3,2,1,0:T(8,128)(2,1)S(1)}, u32[]{:S(2)}, u32[]{:S(2)}) collective-permute-start(bf16[1,1,1,96,768]{4,3,2,1,0:T(8,128)(2,1)S(1)} %constant_dynamic-slice_fusion.13), channel_id=1, source_target_pairs={{0,16},{4,20},{8,24},{12,28},{16,0},{20,4},{24,8},{28,12},{1,17},{... | collective-permute-start | bytes 442376 | tf_op jit(solution)/shard_map/ppermute | solution.py:191
  (65 other events, 239.1 us)
Sparse Core Ops, SparseCore 0:
  194.1 129.7 all-reduce.12
